TPU v7x, 32 devices: a whole 2x2x4 slice. The times are simulated.
32 devices in a mesh: lat: 4 (over y, core), lon: 8 (over z, x).
Axes of the slice: x: 2, y: 2, z: 4, core: 2. Of those that a mesh axis runs over, the one named last changes fastest.
Arguments:
- depth: float32 [32, 8192], P('lat', 'lon'), may hold values from 0.5 to 4
- friction: float32 [32, 8192], P('lat', 'lon'), may hold values from 0.2 to 2
- ocean_mask: int32 [32, 8192], P('lat', 'lon'), may hold values 0 or 1
- forcing: float32 [16, 32, 8192], P(None, 'lat', 'lon'), may hold values from -24 to 24
- tile_route: int32 [512, 1], P(('lat', 'lon')), may hold values from 0 to 7; in each aligned block of 16 rows (0 to 15, 16 to 31, ...) at most 2 rows name the same one
- tile_block: int32 [512], P(('lat', 'lon')), may hold values from 0 to 63
- obs_cell: int32 [512, 128], P(('lat', 'lon')), may hold values from 0 to 127
- obs_time: float32 [512, 128], P(('lat', 'lon')), may hold values from 0 to 720
- obs_value: float32 [512, 128], P(('lat', 'lon')), may hold values from -6 to 6
- obs_weight: float32 [512, 128], P(('lat', 'lon')), may hold values from 0.5 to 4
Outputs:
- elevation: float32 [16, 32, 8192], P(None, 'lat', 'lon')
- residual: float32 [16, 32, 8192], P(None, 'lat', 'lon')
Inputs may be any that keep to these rules, and one draw needn't show every extreme that they name: `tile_route`: among the 16 tiles of one device at most 2 name the same owner, and in some device exactly 2 do.
All inputs are finite; a program needn't handle non-finite values. No bound on the sum of `ocean_mask` on one device may be relied on, other than what follows from the above.
Results may differ from a plain program's by a relative error of at most 0.0007.
Values sent between devices are 32-bit elements; how exact they have to be, the bound alone decides.
A program may use at most 64 MiB of HBM per device.

v0:
```python
import functools
import math

import jax
import jax.numpy as jnp
import numpy as np
from jax import lax
from jax.experimental import pallas as pl
from jax.experimental.pallas import tpu as pltpu
from jax.sharding import PartitionSpec as P

BLOCK = 128
CAP = 2
ITERS = 3
OUTER = 2
STEPS = ITERS * OUTER
MESH = pl.DeviceIdType.MESH
OMEGA_DEGREES = (28.984104, 30.0, 28.43973, 30.082137, 15.041069, 13.943036, 14.958931, 13.398661)
RATES = np.array(OMEGA_DEGREES, np.float32) * np.float32(math.pi / 180.0)
STIFF = np.float32(0.2) * (RATES / RATES[0]) ** 2


def sin_cos(angle):
    turn = jnp.floor(angle * (2.0 / math.pi) + 0.5)
    x = ((angle - turn * 1.5703125) - turn * 4.837512969970703125e-4) - turn * 7.54978995489188216e-8
    z = x * x
    s = ((-1.9515295891e-4 * z + 8.3321608736e-3) * z - 1.6666654611e-1) * z * x + x
    c = ((2.443315711809948e-5 * z - 1.388731625493765e-3) * z + 4.166664568298827e-2) * z * z - 0.5 * z + 1.0
    quarter = turn.astype(jnp.int32)
    odd = (quarter & 1) == 1
    sine = jnp.where(odd, c, s)
    cosine = jnp.where(odd, s, c)
    sine = jnp.where((quarter & 2) == 2, -sine, sine)
    cosine = jnp.where(((quarter + 1) & 2) == 2, -cosine, cosine)
    return sine, cosine


def kernel(
    nlat, nlon,
    route, tblk, *refs,
):
    sources, refs = refs[:8], refs[8:]
    landed = refs[-9:-1]
    work(nlat, nlon, sources, refs[-1], route, tblk, *landed, *refs[:-9])


def work(
    nlat, nlon, sources, load,
    route, tblk, depth, fric, mask, forc, ocell, otime, oval, oweight,
    x_out, r_out,
    dw, dwn, dws, dwe, dww, wetb, wetfric, coef, diag,
    payf, payi, outf, outi, inf, ini, plan, splan, mats, oslot,
    d, db, x, r, q, hd, hx, hr, hq, pk, sum_a, part_row, ready,
    hs, hrv, as_, ar, os_, orv, ds_, dr, loc,
):
    rows, cols = depth.shape
    nblk = cols // BLOCK
    slots = nlon * CAP
    tiles = otime.shape[0]
    me_lat = lax.axis_index("lat")
    me_lon = lax.axis_index("lon")
    north, south = lax.rem(me_lat + 1, nlat), lax.rem(me_lat + nlat - 1, nlat)
    east, west = lax.rem(me_lon + 1, nlon), lax.rem(me_lon + nlon - 1, nlon)

    loads = [
        pltpu.make_async_copy(src, dst, load.at[k])
        for k, (src, dst) in enumerate(zip(sources, (depth, fric, mask, forc, ocell, otime, oval, oweight)))
    ]
    for c in loads:
        c.start()
    barrier = pltpu.get_barrier_semaphore()
    for k in range(1, nlon):
        pl.semaphore_signal(barrier, inc=1, device_id={"lon": lax.rem(me_lon + k, nlon)}, device_id_type=MESH)
    for k in range(1, nlat):
        pl.semaphore_signal(barrier, inc=1, device_id={"lat": lax.rem(me_lat + k, nlat)}, device_id_type=MESH)

    def remote(src, dst, send, recv, where):
        return pltpu.make_async_remote_copy(
            src_ref=src, dst_ref=dst, send_sem=send, recv_sem=recv, device_id=where, device_id_type=MESH
        )

    lane = lax.broadcasted_iota(jnp.int32, (1, BLOCK), 1)
    lane8 = lax.broadcasted_iota(jnp.int32, (8, BLOCK), 1)
    sub8 = lax.broadcasted_iota(jnp.int32, (8, BLOCK), 0)

    for c in loads:
        c.wait()
    wet = mask[...].astype(jnp.float32)
    dw[...] = depth[...] * wet

    for t in range(tiles):
        payf[t, 0:1] = otime[t : t + 1]
        payf[t, 1:2] = oval[t : t + 1]
        payf[t, 2:3] = oweight[t : t + 1]
        payf[t, 3:4] = jnp.zeros((1, BLOCK), jnp.float32)
        payi[t] = jnp.broadcast_to(ocell[t : t + 1] + tblk[t] * BLOCK, (8, BLOCK))
    payf[tiles] = jnp.zeros((8, BLOCK), jnp.float32)
    payi[tiles] = jnp.zeros((8, BLOCK), jnp.int32)

    def pick(p, carry):
        first, second = jnp.int32(tiles), jnp.int32(tiles)
        for t in reversed(range(tiles)):
            hit = route[t] == p
            second = jnp.where(hit, first, second)
            first = jnp.where(hit, jnp.int32(t), first)
        one, two = payf[first], payf[second]
        outf[p] = jnp.concatenate([one[0:4], two[0:4]], axis=0)
        outi[p] = jnp.where(sub8 == 0, payi[first], payi[second])
        return carry

    lax.fori_loop(0, nlon, pick, 0)
    pl.semaphore_wait(barrier, nlon + nlat - 2)
    for k in range(1, nlat):
        pl.semaphore_signal(ready, inc=1, device_id={"lat": lax.rem(me_lat + k, nlat)}, device_id_type=MESH)

    first_copies = [
        remote(dw, dws, ds_.at[0], dr.at[0], {"lat": north}),
        remote(dw, dwn, ds_.at[1], dr.at[1], {"lat": south}),
        remote(dw.at[:, pl.ds(0, BLOCK)], dwe, ds_.at[2], dr.at[2], {"lon": west}),
        remote(dw.at[:, pl.ds(cols - BLOCK, BLOCK)], dww, ds_.at[3], dr.at[3], {"lon": east}),
    ]

    def obs_copy(k):
        peer = lax.rem(me_lon + k, nlon)
        return [
            remote(outf.at[peer], inf.at[me_lon], os_.at[0, peer], orv.at[0, me_lon], {"lon": peer}),
            remote(outi.at[peer], ini.at[me_lon], os_.at[1, peer], orv.at[1, me_lon], {"lon": peer}),
        ]

    def obs_wait(k):
        peer = lax.rem(me_lon + k, nlon)
        remote(outf.at[peer], inf.at[peer], os_.at[0, peer], orv.at[0, peer], {"lon": peer}).wait_recv()
        remote(outi.at[peer], ini.at[peer], os_.at[1, peer], orv.at[1, peer], {"lon": peer}).wait_recv()

    obs_sends = [c for k in range(1, nlon) for c in obs_copy(k)]
    for c in obs_sends:
        c.start()
    for c in first_copies:
        c.start()
    inf[me_lon] = outf[me_lon]
    ini[me_lon] = outi[me_lon]

    for cb in range(nblk):
        at = pl.ds(cb * BLOCK, BLOCK)
        for h in range(2):
            r[pl.ds(1, rows), h, :, at] = jnp.swapaxes(forc[h, :, :, at], 0, 1)
    x[...] = jnp.zeros_like(x)
    hx[...] = jnp.zeros_like(hx)
    oslot[slots] = jnp.zeros((2, 8, BLOCK), jnp.float32)

    for c in first_copies:
        c.wait_recv()
    a = dw[...]
    colid = lax.broadcasted_iota(jnp.int32, (rows, cols), 1)
    rowid = lax.broadcasted_iota(jnp.int32, (rows, cols), 0)
    keep_n = (me_lat < nlat - 1).astype(jnp.float32)
    keep_s = (me_lat > 0).astype(jnp.float32)

    def harmonic(first, second):
        return 2.0 * first * second / jnp.maximum(first + second, 0.5)

    side = harmonic(a, jnp.where(colid == cols - 1, dwe[:, 0:1], pltpu.roll(a, cols - 1, 1)))
    total = side
    for row in range(rows):
        coef[0, row] = jnp.broadcast_to(side[row : row + 1], (8, cols))
    side = harmonic(a, jnp.where(colid == 0, dww[:, BLOCK - 1 : BLOCK], pltpu.roll(a, 1, 1)))
    total = total + side
    for row in range(rows):
        coef[1, row] = jnp.broadcast_to(side[row : row + 1], (8, cols))
    side = harmonic(a, jnp.where(rowid == rows - 1, dwn[0:1, :] * keep_n, pltpu.roll(a, rows - 1, 0)))
    total = total + side
    for row in range(rows):
        coef[2, row] = jnp.broadcast_to(side[row : row + 1], (8, cols))
    side = harmonic(a, jnp.where(rowid == 0, dws[rows - 1 : rows, :] * keep_s, pltpu.roll(a, 1, 0)))
    total = total + side
    for row in range(rows):
        coef[3, row] = jnp.broadcast_to(side[row : row + 1], (8, cols))
    stiff = jnp.zeros((8, 1), jnp.float32)
    rate = jnp.zeros((8, BLOCK), jnp.float32)
    sub1 = lax.broadcasted_iota(jnp.int32, (8, 1), 0)
    for c in range(8):
        stiff = jnp.where(sub1 == c, float(STIFF[c]), stiff)
        rate = jnp.where(sub8 == c, float(RATES[c]), rate)
    drag = fric[...]
    total = total + wet * drag + (1.0 - wet)
    for row in range(rows):
        wide = jnp.broadcast_to(wet[row : row + 1], (8, cols))
        wetb[row] = wide
        wetfric[row] = wide * jnp.broadcast_to(drag[row : row + 1], (8, cols))
        diag[row] = wide * stiff + jnp.broadcast_to(total[row : row + 1], (8, cols))

    for k in range(1, nlon):
        obs_wait(k)
    rep = jnp.full((1, BLOCK), slots, jnp.int32)
    homes = jnp.full((1, BLOCK), -1, jnp.int32)
    for s in reversed(range(slots)):
        home = ini[s // CAP, pl.ds(s % CAP, 1), :] >> 7
        rep = jnp.where(home == lane, s, rep)
        homes = jnp.where(lane == s, home, homes)
    chain = jnp.full((1, BLOCK), slots, jnp.int32)
    for s in reversed(range(slots)):
        home = ini[s // CAP, pl.ds(s % CAP, 1), :] >> 7
        chain = jnp.where((home == homes) & (lane < s), s, chain)
    plan[...] = jnp.where(
        sub8 == 0,
        jnp.broadcast_to(homes, (8, BLOCK)),
        jnp.where(sub8 == 1, jnp.broadcast_to(chain, (8, BLOCK)), jnp.broadcast_to(rep, (8, BLOCK))),
    )
    to_scalars = pltpu.make_async_copy(plan, splan, loc.at[0])
    to_scalars.start()

    cells = lax.broadcasted_iota(jnp.int32, (BLOCK, BLOCK), 0)

    def build(o, carry):
        for k in range(CAP):
            times = inf[o, pl.ds(4 * k, 1), :]
            value = inf[o, pl.ds(4 * k + 1, 1), :]
            weight = inf[o, pl.ds(4 * k + 2, 1), :]
            cell = ini[o, pl.ds(k, 1), :] & (BLOCK - 1)
            sine, cosine = sin_cos(rate * times)
            basis = (cosine, sine)
            weighted = (weight * cosine, weight * sine)
            parts = []
            for h in range(2):
                for c in range(8):
                    one = weighted[h][c : c + 1]
                    parts.append(one * basis[0])
                    parts.append(one * basis[1])
            parts.append(weighted[0] * value)
            parts.append(weighted[1] * value)
            terms = jnp.concatenate(parts, axis=0)
            high = terms.astype(jnp.bfloat16)
            low = (terms - high.astype(jnp.float32)).astype(jnp.bfloat16)
            hot = (cells == cell).astype(jnp.float32).astype(jnp.bfloat16)
            mats[o * CAP + k] = lax.dot_general(
                jnp.concatenate([high, low], axis=1),
                jnp.concatenate([hot, hot], axis=1),
                (((1,), (1,)), ((), ())),
                preferred_element_type=jnp.float32,
            )
        return carry

    lax.fori_loop(0, nlon, build, 0)
    to_scalars.wait()

    def first_slots(i, carry):
        s = slots - 1 - i
        after = oslot[splan[1, s]]
        oslot[s] = mats[s, 256:272, :].reshape(2, 8, BLOCK) + after
        return carry

    lax.fori_loop(0, slots, first_slots, 0)

    def pack(row, col, value, packed):
        shift = row if col == 0 else row + 1
        moved = pltpu.roll(value, shift, 2)
        return jnp.where(lane8 == row, moved, packed)

    zero = jnp.zeros((2, 8, BLOCK), jnp.float32)

    def start_rhs(row, carry):
        lo, hi = carry
        for cb in range(nblk):
            at = pl.ds(cb * BLOCK, BLOCK)
            v = wetb[row, :, at] * r[row + 1, :, :, at] + oslot[splan[2, row * nblk + cb]]
            r[row + 1, :, :, at] = v
            q[STEPS, row + 1, :, :, at] = v
            db[(row + 1) * nblk + cb] = v
            if cb == 0:
                lo = pack(row, 0, v, lo)
            if cb == nblk - 1:
                hi = pack(row, 1, v, hi)
        return lo, hi

    lo, hi = lax.fori_loop(0, rows, start_rhs, (zero, zero))
    pk[STEPS, 0] = lo
    pk[STEPS, 1] = hi

    def halo(i):
        return [
            remote(q.at[i, 1], q.at[i, rows + 1], hs.at[i, 0], hrv.at[i, 0], {"lat": south}),
            remote(q.at[i, rows], q.at[i, 0], hs.at[i, 1], hrv.at[i, 1], {"lat": north}),
            remote(pk.at[i, 0], hq.at[i, 1], hs.at[i, 2], hrv.at[i, 2], {"lon": west}),
            remote(pk.at[i, 1], hq.at[i, 0], hs.at[i, 3], hrv.at[i, 3], {"lon": east}),
        ]

    def begin(i):
        for c in halo(i):
            c.start()
        d[pl.ds(1, rows)] = r[pl.ds(1, rows)]
        for c in halo(i):
            c.wait()
        for edge in (0, rows + 1):
            d[edge] = q[i, edge]
            r[edge] = q[i, edge]
        hd[...] = hq[i]
        hr[...] = hq[i]

    me = me_lat * nlon + me_lon
    count = nlat * nlon

    def sum_copy(i, k):
        peer = lax.rem(me + k, count)
        where = {"lat": peer // nlon, "lon": lax.rem(peer, nlon)}
        return remote(part_row.at[i], sum_a.at[i, pl.ds(me, 1)], as_.at[i], ar.at[i], where)

    def sum_wait(i):
        whole = sum_a.at[i, pl.ds(0, count - 1)]
        return remote(whole, whole, as_.at[i], ar.at[i], {"lat": south})

    def all_sum(i, part):
        part = part + pltpu.roll(part, 64, 1)
        part = part + pltpu.roll(part, 32, 1)
        row = jnp.sum(jnp.where(lane8 >> 5 == sub8, part, 0.0), axis=0, keepdims=True)
        part_row[i] = row
        sum_a[i, pl.ds(me, 1)] = row

        def send(k, carry):
            sum_copy(i, k).start()
            return carry

        lax.fori_loop(1, count, send, 0, unroll=True)
        sum_wait(i).wait_recv()
        total = jnp.sum(sum_a[i], axis=0, keepdims=True)
        return jnp.sum(jnp.where(lane8 >> 5 == sub8, total, 0.0), axis=1, keepdims=True)

    def sides(ref, halos, row):
        v = [ref[row + 1, :, :, pl.ds(cb * BLOCK, BLOCK)] for cb in range(nblk)]
        to_west = [pltpu.roll(b, BLOCK - 1, 2) for b in v]
        to_west.append(pltpu.roll(halos[1], BLOCK - 1 - row, 2))
        to_east = [pltpu.roll(halos[0], BLOCK - row, 2)] + [pltpu.roll(b, 1, 2) for b in v]
        e = [jnp.where(lane8 == BLOCK - 1, to_west[cb + 1], to_west[cb]) for cb in range(nblk)]
        w = [jnp.where(lane8 == 0, to_east[cb], to_east[cb + 1]) for cb in range(nblk)]
        return v, e, w

    def step(i, carry):
        def slot(j, carry):
            s = slots - 1 - j
            after = oslot[splan[1, s]]
            v = db[splan[0, s] + nblk]
            acc = [after, zero]
            for c in range(16):
                m = mats[s, 16 * c : 16 * c + 16, :].reshape(2, 8, BLOCK)
                acc[c % 2] = acc[c % 2] + m * v[c // 8, c % 8 : c % 8 + 1, :]
            oslot[s] = acc[0] + acc[1]
            return carry

        lax.fori_loop(0, slots, slot, 0)

        def line(row, carry):
            lo, hi, rr, rq, dq, qq = carry
            v, e, w = sides(d, hd, row)
            for cb in range(nblk):
                at = pl.ds(cb * BLOCK, BLOCK)
                image = (
                    diag[row, :, at] * v[cb]
                    - coef[0, row, :, at] * e[cb]
                    - coef[1, row, :, at] * w[cb]
                    - coef[2, row, :, at] * d[row + 2, :, :, at]
                    - coef[3, row, :, at] * d[row, :, :, at]
                    + oslot[splan[2, row * nblk + cb]]
                )
                q[i, row + 1, :, :, at] = image
                res = r[row + 1, :, :, at]
                rr = rr + res * res
                rq = rq + res * image
                dq = dq + v[cb] * image
                qq = qq + image * image
                if cb == 0:
                    lo = pack(row, 0, image, lo)
                if cb == nblk - 1:
                    hi = pack(row, 1, image, hi)
            return lo, hi, rr, rq, dq, qq

        lo, hi, *sums = lax.fori_loop(0, rows, line, (zero,) * 6)
        pk[i, 0] = lo
        pk[i, 1] = hi
        part = jnp.zeros((8, BLOCK), jnp.float32)
        for k, s in enumerate(sums):
            part = jnp.where(sub8 == k, jnp.sum(s[0] + s[1], axis=0, keepdims=True), part)
        more = lax.rem(i, ITERS) < ITERS - 1

        @pl.when(more)
        def _():
            for c in halo(i):
                c.start()

        whole = all_sum(i, part)
        rr, rq, dq, qq = (whole[k : k + 1] for k in range(4))
        size = rr / dq
        beta = (rr - 2.0 * size * rq + size * size * qq) / rr

        @pl.when(more)
        def _():
            for c in halo(i):
                c.wait()

        def update(row, carry):
            for cb in range(nblk):
                at = pl.ds(cb * BLOCK, BLOCK)
                old = d[row, :, :, at]
                x[row, :, :, at] = x[row, :, :, at] + size * old
                res = r[row, :, :, at] - size * q[i, row, :, :, at]
                r[row, :, :, at] = res
                new = res + beta * old
                d[row, :, :, at] = new
                db[row * nblk + cb] = new
            return carry

        lax.fori_loop(0, rows + 2, update, 0)
        hx[...] = hx[...] + size * hd[...]
        hr[...] = hr[...] - size * hq[i]
        hd[...] = hr[...] + beta * hd[...]
        sum_wait(i).wait_send()
        return carry

    begin(STEPS)
    pl.semaphore_wait(ready, nlat - 1)
    for c in obs_sends + first_copies:
        c.wait_send()
    lax.fori_loop(0, ITERS, step, 0)

    def friction(row, carry):
        lo, hi = carry
        v, e, _ = sides(x, hx, row)
        for cb in range(nblk):
            at = pl.ds(cb * BLOCK, BLOCK)
            flux_e = coef[0, row, :, at] * (e[cb] - v[cb])
            flux_n = coef[2, row, :, at] * (x[row + 2, :, :, at] - v[cb])
            square = flux_e * flux_e + flux_n * flux_n
            speed = jnp.sum(square[0] + square[1], axis=0, keepdims=True)
            extra = wetfric[row, :, at] * (jnp.sqrt(1.0 + speed / 16.0) - 1.0)
            diag[row, :, at] = diag[row, :, at] + extra
            res = r[row + 1, :, :, at] - extra * v[cb]
            r[row + 1, :, :, at] = res
            q[STEPS + 1, row + 1, :, :, at] = res
            db[(row + 1) * nblk + cb] = res
            if cb == 0:
                lo = pack(row, 0, res, lo)
            if cb == nblk - 1:
                hi = pack(row, 1, res, hi)
        return lo, hi

    lo, hi = lax.fori_loop(0, rows, friction, (zero, zero))
    pk[STEPS + 1, 0] = lo
    pk[STEPS + 1, 1] = hi
    begin(STEPS + 1)
    lax.fori_loop(ITERS, STEPS, step, 0)

    for cb in range(nblk):
        at = pl.ds(cb * BLOCK, BLOCK)
        for h in range(2):
            x_out[h, :, :, at] = jnp.swapaxes(x[pl.ds(1, rows), h, :, at], 0, 1)
            r_out[h, :, :, at] = jnp.swapaxes(r[pl.ds(1, rows), h, :, at], 0, 1)


def shards(nlat, nlon, depth, friction, ocean_mask, forcing, tile_route, tile_block, obs_cell, obs_time, obs_value, obs_weight):
    channels, rows, cols = forcing.shape
    slots = nlon * CAP
    nblk, tiles = cols // BLOCK, obs_time.shape[0]
    f32, i32 = jnp.float32, jnp.int32
    vmem = pl.BlockSpec(memory_space=pltpu.VMEM)
    smem = pl.BlockSpec(memory_space=pltpu.SMEM)
    field = (rows + 2, 2, 8, cols)
    dma = pltpu.SemaphoreType.DMA
    scratch = [
        pltpu.VMEM((rows, cols), f32),
        pltpu.VMEM((rows, cols), f32),
        pltpu.VMEM((rows, cols), f32),
        pltpu.VMEM((rows, BLOCK), f32),
        pltpu.VMEM((rows, BLOCK), f32),
        pltpu.VMEM((rows, 8, cols), f32),
        pltpu.VMEM((rows, 8, cols), f32),
        pltpu.VMEM((4, rows, 8, cols), f32),
        pltpu.VMEM((rows, 8, cols), f32),
        pltpu.VMEM((tiles + 1, 8, BLOCK), f32),
        pltpu.VMEM((tiles + 1, 8, BLOCK), i32),
        pltpu.VMEM((nlon, 8, BLOCK), f32),
        pltpu.VMEM((nlon, 8, BLOCK), i32),
        pltpu.VMEM((nlon, 8, BLOCK), f32),
        pltpu.VMEM((nlon, 8, BLOCK), i32),
        pltpu.VMEM((8, BLOCK), i32),
        pltpu.SMEM((8, BLOCK), i32),
        pltpu.VMEM((slots, 272, BLOCK), f32),
        pltpu.VMEM((slots + 1, 2, 8, BLOCK), f32),
        pltpu.VMEM(field, f32),
        pltpu.VMEM(((rows + 2) * nblk, 2, 8, BLOCK), f32),
        pltpu.VMEM(field, f32),
        pltpu.VMEM(field, f32),
        pltpu.VMEM((STEPS + 2,) + field, f32),
        pltpu.VMEM((2, 2, 8, BLOCK), f32),
        pltpu.VMEM((2, 2, 8, BLOCK), f32),
        pltpu.VMEM((2, 2, 8, BLOCK), f32),
        pltpu.VMEM((STEPS + 2, 2, 2, 8, BLOCK), f32),
        pltpu.VMEM((STEPS + 2, 2, 2, 8, BLOCK), f32),
        pltpu.VMEM((STEPS, nlat * nlon, BLOCK), f32),
        pltpu.VMEM((STEPS, 1, BLOCK), f32),
        pltpu.SemaphoreType.REGULAR,
        dma((STEPS + 2, 4)),
        dma((STEPS + 2, 4)),
        dma((STEPS,)),
        dma((STEPS,)),
        dma((2, nlon)),
        dma((2, nlon)),
        dma((4,)),
        dma((4,)),
        dma((1,)),
        pltpu.VMEM((rows, cols), f32),
        pltpu.VMEM((rows, cols), f32),
        pltpu.VMEM((rows, cols), i32),
        pltpu.VMEM((2, channels // 2, rows, cols), f32),
        pltpu.VMEM((tiles, BLOCK), i32),
        pltpu.VMEM((tiles, BLOCK), f32),
        pltpu.VMEM((tiles, BLOCK), f32),
        pltpu.VMEM((tiles, BLOCK), f32),
        dma((8,)),
    ]
    shape = jax.ShapeDtypeStruct((2, channels // 2, rows, cols), f32)
    x, r = pl.pallas_call(
        functools.partial(kernel, nlat, nlon),
        out_shape=(shape, shape),
        in_specs=[smem, smem] + [pl.BlockSpec(memory_space=pltpu.HBM)] * 8,
        out_specs=(vmem, vmem),
        scratch_shapes=scratch,
        compiler_params=pltpu.CompilerParams(
            collective_id=0, has_side_effects=True, vmem_limit_bytes=62 * 2**20
        ),
    )(
        tile_route.reshape(-1), tile_block, depth, friction, ocean_mask, forcing.reshape(2, channels // 2, rows, cols),
        obs_cell, obs_time, obs_value, obs_weight,
    )
    return x.reshape(forcing.shape), r.reshape(forcing.shape)


def solution(mesh):
    tile = P(("lat", "lon"), None)
    grid = P("lat", "lon")
    in_specs = (grid, grid, grid, P(None, "lat", "lon"), tile, P(("lat", "lon")), tile, tile, tile, tile)
    out_specs = (P(None, "lat", "lon"), P(None, "lat", "lon"))
    body = functools.partial(shards, mesh.shape["lat"], mesh.shape["lon"])
    return jax.shard_map(body, mesh=mesh, in_specs=in_specs, out_specs=out_specs, check_vma=False)
```

profile of v0, /device:TPU:0, one launch (start us, length us, event | category | flops | bytes accessed | tf_op | source)
XLA Modules:
  0.0 69.5 jit_solution(18184341197597767929)
XLA Ops:
  0.6 66.1 %shard_map.113 = (f32[2,8,8,1024]{3,2,1,0:T(8,128)}, f32[2,8,8,1024]{3,2,1,0:T(8,128)}) custom-call(s32[16]{0:T(128)} %bitcast.7, s32[16]{0:T(128)} %tblk.1, f32[8,1024]{1,0:T(8,128)} %refs_0_.1, f32[8,1024]{1,0:T(8,128)} %refs_1_.1, s32[8,1024]{1,0:T(8,128)} %refs_2_.1, f32[2,8,8,1024]{3,2,1,0:T(8,128)} %bitcast.4, s32[16,128]{1,0:T(8,128)} %refs_4_.1, ...), custom_call_target="tpu_custom_call" | custom-call | tf_op jit(solution)/shard_map/pallas_call | solution.py:519
  66.7 0.0 copy-start
  66.7 1.9 %copy.14 = f32[16,8,1024]{2,1,0:T(8,128)} copy(f32[16,8,1024]{2,1,0:T(8,128)} %bitcast.6) | data formatting | bytes 1048576
  68.7 0.0 copy-done
  68.7 0.8 %copy.15 = f32[16,8,1024]{2,1,0:T(8,128)} copy(f32[16,8,1024]{2,1,0:T(8,128)S(1)} %bitcast.5) | data formatting | bytes 1048576
Async XLA Ops:
  66.7 2.0 %copy-start = (f32[2,8,8,1024]{3,2,1,0:T(8,128)S(1)}, f32[2,8,8,1024]{3,2,1,0:T(8,128)}, u32[]{:S(2)}) copy-start(f32[2,8,8,1024]{3,2,1,0:T(8,128)} %get-tuple-element.5) | copy-start | bytes 1572868
where the time goes:
time: 69.6 us; the launch traced here: 69.5 us
  Pallas kernels  66.1 us (95%)
  local copies, waits for them, and re-layouts  2.74 us (4%)
    pallas_call x1, Pallas kernels, shards(): pl.pallas_call(functools.partial(kernel, nlat, nlon), out_shape=(shape, s...  66.1 us
    unnamed x4, local copies, waits for them, and re-layouts  2.74 us

commit v1 on v0

v1 whole, which is shorter than its diff:
```python
import functools
import math

import jax
import jax.numpy as jnp
import numpy as np
from jax import lax
from jax.experimental import pallas as pl
from jax.experimental.pallas import tpu as pltpu
from jax.sharding import PartitionSpec as P

BLOCK = 128
CAP = 2
ITERS = 3
OUTER = 2
SUMS = ITERS * OUTER
MESH = pl.DeviceIdType.MESH
OMEGA_DEGREES = (28.984104, 30.0, 28.43973, 30.082137, 15.041069, 13.943036, 14.958931, 13.398661)
RATES = np.array(OMEGA_DEGREES, np.float32) * np.float32(math.pi / 180.0)
STIFF = np.float32(0.2) * (RATES / RATES[0]) ** 2


def sin_cos(angle):
    turn = jnp.floor(angle * (2.0 / math.pi) + 0.5)
    x = ((angle - turn * 1.5703125) - turn * 4.837512969970703125e-4) - turn * 7.54978995489188216e-8
    z = x * x
    s = ((-1.9515295891e-4 * z + 8.3321608736e-3) * z - 1.6666654611e-1) * z * x + x
    c = ((2.443315711809948e-5 * z - 1.388731625493765e-3) * z + 4.166664568298827e-2) * z * z - 0.5 * z + 1.0
    quarter = turn.astype(jnp.int32)
    odd = (quarter & 1) == 1
    sine = jnp.where(odd, c, s)
    cosine = jnp.where(odd, s, c)
    sine = jnp.where((quarter & 2) == 2, -sine, sine)
    cosine = jnp.where(((quarter + 1) & 2) == 2, -cosine, cosine)
    return sine, cosine


def kernel(
    nlat, nlon,
    route_in, tblk_in, depth_in, fric_in, mask_in, forc_in, ocell_in, otime_in, oval_in, oweight_in,
    x_out, p_out, r_out, q_out, size_out,
    route, tblk, depth, fric, mask, forc, ocell, otime, oval, oweight,
    dw, dwn, dws, dwe, dww, wetfric, coef, diag,
    pay, payi, outf, outi, inf, ini, plan, splan, waves, mats, oslot,
    field, seen, r1, p1, q1, z1, r2, p2, q2, x, turned,
    pk, hq, hq1, hx, hp, sum_a, part_row, ready,
    load, hs, hrv, as_, ar, os_, orv, ds_, dr, loc, out_sem,
):
    rows, cols = depth.shape
    nblk = cols // BLOCK
    slots = nlon * CAP
    tiles = otime.shape[0]
    me_lat = lax.axis_index("lat")
    me_lon = lax.axis_index("lon")
    north, south = lax.rem(me_lat + 1, nlat), lax.rem(me_lat + nlat - 1, nlat)
    east, west = lax.rem(me_lon + 1, nlon), lax.rem(me_lon + nlon - 1, nlon)
    me = me_lat * nlon + me_lon
    count = nlat * nlon

    barrier = pltpu.get_barrier_semaphore()
    for k in range(1, nlon):
        pl.semaphore_signal(barrier, inc=1, device_id={"lon": lax.rem(me_lon + k, nlon)}, device_id_type=MESH)
    for k in range(1, nlat):
        pl.semaphore_signal(barrier, inc=1, device_id={"lat": lax.rem(me_lat + k, nlat)}, device_id_type=MESH)
    pairs = [
        (route_in, route), (tblk_in, tblk), (ocell_in, ocell), (otime_in, otime), (oval_in, oval),
        (oweight_in, oweight), (depth_in, depth), (mask_in, mask), (fric_in, fric), (forc_in, forc),
    ]
    loads = [pltpu.make_async_copy(src, dst, load.at[k]) for k, (src, dst) in enumerate(pairs)]
    for c in loads:
        c.start()

    def remote(src, dst, send, recv, where):
        return pltpu.make_async_remote_copy(
            src_ref=src, dst_ref=dst, send_sem=send, recv_sem=recv, device_id=where, device_id_type=MESH
        )

    lane = lax.broadcasted_iota(jnp.int32, (1, BLOCK), 1)
    lane8 = lax.broadcasted_iota(jnp.int32, (8, BLOCK), 1)
    sub8 = lax.broadcasted_iota(jnp.int32, (8, BLOCK), 0)
    zero = jnp.zeros((2, 8, BLOCK), jnp.float32)

    for c in loads[:8]:
        c.wait()
    wet = mask[...].astype(jnp.float32)
    dw[...] = depth[...] * wet

    for t in range(tiles):
        pay[t] = jnp.concatenate([otime[t : t + 1], oval[t : t + 1], oweight[t : t + 1], oval[t : t + 1]] * 2, axis=0)
        payi[t] = jnp.broadcast_to(ocell[t : t + 1] + tblk[t] * BLOCK, (8, BLOCK))
    pay[tiles] = jnp.zeros((8, BLOCK), jnp.float32)
    payi[tiles] = jnp.zeros((8, BLOCK), jnp.int32)

    def pick(p, carry):
        first, second = jnp.int32(tiles), jnp.int32(tiles)
        for t in reversed(range(tiles)):
            hit = route[t] == p
            second = jnp.where(hit, first, second)
            first = jnp.where(hit, jnp.int32(t), first)
        outf[p] = jnp.where(sub8 < 4, pay[first], pay[second])
        outi[p] = jnp.where(sub8 == 0, payi[first], payi[second])
        return carry

    lax.fori_loop(0, nlon, pick, 0)
    pl.semaphore_wait(barrier, nlon + nlat - 2)

    def obs_copy(k):
        peer = lax.rem(me_lon + k, nlon)
        return [
            remote(outf.at[peer], inf.at[me_lon], os_.at[0, peer], orv.at[0, me_lon], {"lon": peer}),
            remote(outi.at[peer], ini.at[me_lon], os_.at[1, peer], orv.at[1, me_lon], {"lon": peer}),
        ]

    def obs_wait(k):
        peer = lax.rem(me_lon + k, nlon)
        remote(outf.at[peer], inf.at[peer], os_.at[0, peer], orv.at[0, peer], {"lon": peer}).wait_recv()
        remote(outi.at[peer], ini.at[peer], os_.at[1, peer], orv.at[1, peer], {"lon": peer}).wait_recv()

    obs_sends = [c for k in range(1, nlon) for c in obs_copy(k)]
    for c in obs_sends:
        c.start()
    first_copies = [
        remote(dw.at[:, pl.ds(0, BLOCK)], dwe, ds_.at[2], dr.at[2], {"lon": west}),
        remote(dw.at[:, pl.ds(cols - BLOCK, BLOCK)], dww, ds_.at[3], dr.at[3], {"lon": east}),
        remote(dw, dws, ds_.at[0], dr.at[0], {"lat": north}),
        remote(dw, dwn, ds_.at[1], dr.at[1], {"lat": south}),
    ]
    for c in first_copies:
        c.start()
    for k in range(1, nlat):
        pl.semaphore_signal(ready, inc=1, device_id={"lat": lax.rem(me_lat + k, nlat)}, device_id_type=MESH)
    inf[me_lon] = outf[me_lon]
    ini[me_lon] = outi[me_lon]
    for c in loads[8:]:
        c.wait()

    for cb in range(nblk):
        at = pl.ds(cb * BLOCK, BLOCK)
        for h in range(2):
            wetted = forc[h, :, :, at] * wet[None, :, cb * BLOCK : cb * BLOCK + BLOCK]
            field[0, pl.ds(1, rows), cb, h] = jnp.swapaxes(wetted, 0, 1)
    oslot[slots] = zero
    mats[slots] = jnp.zeros((256, BLOCK), jnp.float32)
    stiff = jnp.zeros((8, 1), jnp.float32)
    rate = jnp.zeros((8, BLOCK), jnp.float32)
    sub1 = lax.broadcasted_iota(jnp.int32, (8, 1), 0)
    for c in range(8):
        stiff = jnp.where(sub1 == c, float(STIFF[c]), stiff)
        rate = jnp.where(sub8 == c, float(RATES[c]), rate)
    cells = lax.broadcasted_iota(jnp.int32, (BLOCK, BLOCK), 0)

    for k in range(1, nlon):
        obs_wait(k)

    def where_is(s):
        return ini[s // CAP, pl.ds(s % CAP, 1), :]

    rep = jnp.full((1, BLOCK), slots, jnp.int32)
    homes = jnp.full((1, BLOCK), -1, jnp.int32)
    for s in reversed(range(slots)):
        home = where_is(s) >> 7
        rep = jnp.where(home == lane, s, rep)
        homes = jnp.where(lane == s, home, homes)
    chain = jnp.full((1, BLOCK), slots, jnp.int32)
    for s in reversed(range(slots)):
        home = where_is(s) >> 7
        chain = jnp.where((home == homes) & (lane < s), s, chain)
    plan[...] = jnp.where(
        sub8 == 0,
        jnp.broadcast_to(homes, (8, BLOCK)),
        jnp.where(sub8 == 1, jnp.broadcast_to(chain, (8, BLOCK)), jnp.broadcast_to(rep, (8, BLOCK))),
    )
    to_scalars = pltpu.make_async_copy(plan, splan, loc.at[0])
    to_scalars.start()

    def onto_cells(o, k, terms):
        cell = ini[o, pl.ds(k, 1), :] & (BLOCK - 1)
        high = terms.astype(jnp.bfloat16)
        low = (terms - high.astype(jnp.float32)).astype(jnp.bfloat16)
        hot = (cells == cell).astype(jnp.float32).astype(jnp.bfloat16)
        return lax.dot_general(
            jnp.concatenate([high, low], axis=1),
            jnp.concatenate([hot, hot], axis=1),
            (((1,), (1,)), ((), ())),
            preferred_element_type=jnp.float32,
        )

    def values(o, carry):
        for k in range(CAP):
            times = inf[o, pl.ds(4 * k, 1), :]
            scaled = inf[o, pl.ds(4 * k + 2, 1), :] * inf[o, pl.ds(4 * k + 1, 1), :]
            sine, cosine = sin_cos(rate * times)
            waves[o * CAP + k, 0] = cosine
            waves[o * CAP + k, 1] = sine
            terms = jnp.concatenate([cosine * scaled, sine * scaled], axis=0)
            oslot[o * CAP + k] = onto_cells(o, k, terms).reshape(2, 8, BLOCK)
        return carry

    lax.fori_loop(0, nlon, values, 0, unroll=4)
    to_scalars.wait()

    def join_values(i, carry):
        s = slots - 1 - i
        oslot[s] = oslot[s] + oslot[splan[1, s]]
        return carry

    lax.fori_loop(0, slots, join_values, 0)

    def pack(row, col, value, packed):
        shift = row if col == 0 else row + 1
        moved = pltpu.roll(value, shift, 2)
        return jnp.where(lane8 == row, moved, packed)

    def pack_ends(row, first, last, carry):
        return pack(row, 0, first, carry[0]), pack(row, 1, last, carry[1])

    def keep_ends(k, ends):
        pk[k, 0] = ends[0]
        pk[k, 1] = ends[1]

    def start_rhs(row, ends):
        v = []
        for cb in range(nblk):
            v.append(field[0, row + 1, cb] + oslot[splan[2, row * nblk + cb]])
            field[0, row + 1, cb] = v[cb]
            seen[row * nblk + cb] = v[cb]
        return pack_ends(row, v[0], v[-1], ends)

    keep_ends(0, lax.fori_loop(0, rows, start_rhs, (zero, zero)))

    def halo(k):
        return [
            remote(pk.at[k, 0], hq.at[k, 1], hs.at[k, 2], hrv.at[k, 2], {"lon": west}),
            remote(pk.at[k, 1], hq.at[k, 0], hs.at[k, 3], hrv.at[k, 3], {"lon": east}),
            remote(field.at[k, 1], field.at[k, rows + 1], hs.at[k, 0], hrv.at[k, 0], {"lat": south}),
            remote(field.at[k, rows], field.at[k, 0], hs.at[k, 1], hrv.at[k, 1], {"lat": north}),
        ]

    def send_halo(k):
        for c in halo(k):
            c.start()

    def wait_halo(k):
        for c in halo(k):
            c.wait_recv()

    send_halo(0)

    for c in first_copies:
        c.wait_recv()
    a = dw[...]
    colid = lax.broadcasted_iota(jnp.int32, (rows, cols), 1)
    rowid = lax.broadcasted_iota(jnp.int32, (rows, cols), 0)
    keep_n = (me_lat < nlat - 1).astype(jnp.float32)
    keep_s = (me_lat > 0).astype(jnp.float32)

    def harmonic(first, second):
        return 2.0 * first * second / jnp.maximum(first + second, 0.5)

    drag = fric[...]
    total = wet * drag + (1.0 - wet)
    around = (
        lambda: jnp.where(colid == cols - 1, dwe[:, 0:1], pltpu.roll(a, cols - 1, 1)),
        lambda: jnp.where(colid == 0, dww[:, BLOCK - 1 : BLOCK], pltpu.roll(a, 1, 1)),
        lambda: jnp.where(rowid == rows - 1, dwn[0:1, :] * keep_n, pltpu.roll(a, rows - 1, 0)),
        lambda: jnp.where(rowid == 0, dws[rows - 1 : rows, :] * keep_s, pltpu.roll(a, 1, 0)),
    )
    for k in range(4):
        side = harmonic(a, around[k]())
        total = total + side
        for row in range(rows):
            coef[k, row] = jnp.broadcast_to(side[row : row + 1], (8, cols))
    dragged = wet * drag
    for row in range(rows):
        wetfric[row] = jnp.broadcast_to(dragged[row : row + 1], (8, cols))
        wide = jnp.broadcast_to(wet[row : row + 1], (8, cols))
        diag[row] = wide * stiff + jnp.broadcast_to(total[row : row + 1], (8, cols))

    def build(o, carry):
        for k in range(CAP):
            weight = inf[o, pl.ds(4 * k + 2, 1), :]
            basis = (waves[o * CAP + k, 0], waves[o * CAP + k, 1])
            parts = []
            for h in range(2):
                for c in range(8):
                    one = weight * basis[h][c : c + 1]
                    parts.append(one * basis[0])
                    parts.append(one * basis[1])
            mats[o * CAP + k] = onto_cells(o, k, jnp.concatenate(parts, axis=0))
        return carry

    lax.fori_loop(0, nlon, build, 0)

    def join_mats(i, carry):
        s = slots - 1 - i
        mats[s] = mats[s] + mats[splan[1, s]]
        return carry

    lax.fori_loop(0, slots, join_mats, 0)

    def observe():
        def slot(s, carry):
            v = seen[splan[0, s]]
            acc = [zero, zero]
            for c in range(16):
                m = mats[s, 16 * c : 16 * c + 16, :].reshape(2, 8, BLOCK)
                acc[c % 2] = acc[c % 2] + m * v[c // 8, c % 8 : c % 8 + 1, :]
            oslot[s] = acc[0] + acc[1]
            return carry

        lax.fori_loop(0, slots, slot, 0, unroll=2)

    def eastward(v, beyond):
        moved = [pltpu.roll(b, BLOCK - 1, 2) for b in v] + [beyond]
        return [jnp.where(lane8 == BLOCK - 1, moved[cb + 1], moved[cb]) for cb in range(nblk)]

    def westward(v, beyond):
        moved = [beyond] + [pltpu.roll(b, 1, 2) for b in v]
        return [jnp.where(lane8 == 0, moved[cb], moved[cb + 1]) for cb in range(nblk)]

    def from_east(halos, row):
        return pltpu.roll(halos[1], BLOCK - 1 - row, 2)

    def from_west(halos, row):
        return pltpu.roll(halos[0], BLOCK - row, 2)

    def image_row(src, dst, row, east_side, west_side):
        v = [src[row + 1, cb] for cb in range(nblk)]
        e = eastward(v, east_side)
        w = westward(v, west_side)
        for cb in range(nblk):
            at = pl.ds(cb * BLOCK, BLOCK)
            dst[row + 1, cb] = (
                diag[row, :, at] * v[cb]
                - coef[0, row, :, at] * e[cb]
                - coef[1, row, :, at] * w[cb]
                - coef[2, row, :, at] * src[row + 2, cb]
                - coef[3, row, :, at] * src[row, cb]
                + oslot[splan[2, row * nblk + cb]]
            )

    def inside(src, dst):
        def line(row, carry):
            image_row(src, dst, row, zero, zero)
            return carry

        lax.fori_loop(1, rows - 1, line, 0)

    def edges(src, halos, dst):
        for row in (0, rows - 1):
            image_row(src, dst, row, from_east(halos, row), from_west(halos, row))

        def mend(row, carry):
            last = pl.ds(cols - BLOCK, BLOCK)
            dst[row + 1, 0] = dst[row + 1, 0] - coef[1, row, :, pl.ds(0, BLOCK)] * jnp.where(
                lane8 == 0, from_west(halos, row), 0.0
            )
            dst[row + 1, nblk - 1] = dst[row + 1, nblk - 1] - coef[0, row, :, last] * jnp.where(
                lane8 == BLOCK - 1, from_east(halos, row), 0.0
            )
            return carry

        lax.fori_loop(1, rows - 1, mend, 0)

    def sum_copy(i, k):
        peer = lax.rem(me + k, count)
        where = {"lat": peer // nlon, "lon": lax.rem(peer, nlon)}
        return remote(part_row.at[i], sum_a.at[i, pl.ds(me, 1)], as_.at[i], ar.at[i], where)

    def sum_wait(i):
        whole = sum_a.at[i, pl.ds(0, count - 1)]
        return remote(whole, whole, as_.at[i], ar.at[i], {"lat": south})

    def send_sums(i, sums):
        part = jnp.zeros((8, BLOCK), jnp.float32)
        for k, s in enumerate(sums):
            part = jnp.where(sub8 == k, jnp.sum(s[0] + s[1], axis=0, keepdims=True), part)
        part = part + pltpu.roll(part, 64, 1)
        part = part + pltpu.roll(part, 32, 1)
        row = jnp.sum(jnp.where(lane8 >> 5 == sub8, part, 0.0), axis=0, keepdims=True)
        part_row[i] = row
        sum_a[i, pl.ds(me, 1)] = row

        def send(k, carry):
            sum_copy(i, k).start()
            return carry

        lax.fori_loop(1, count, send, 0, unroll=True)

    def take_sums(i):
        sum_wait(i).wait_recv()
        total = jnp.sum(sum_a[i], axis=0, keepdims=True)
        whole = jnp.sum(jnp.where(lane8 >> 5 == sub8, total, 0.0), axis=1, keepdims=True)
        return [jnp.broadcast_to(whole[k : k + 1], (8, BLOCK)) for k in range(4)]

    def beta_of(size, rr, rq, qq):
        return (rr - 2.0 * size * rq + size * size * qq) / rr

    def outer(o):
        k0, kq, kz = 3 * o, 3 * o + 1, 3 * o + 2
        r0, q0, z0 = field.at[k0], field.at[kq], field.at[kz]
        observe()
        inside(r0, q0)
        wait_halo(k0)
        edges(r0, hq.at[k0], q0)

        def first_dots(row, carry):
            ends, rr, rq, qq = carry
            for cb in range(nblk):
                res, image = r0[row + 1, cb], q0[row + 1, cb]
                seen[row * nblk + cb] = image
                rr = rr + res * res
                rq = rq + res * image
                qq = qq + image * image
            return pack_ends(row, q0[row + 1, 0], q0[row + 1, nblk - 1], ends), rr, rq, qq

        ends, *sums = lax.fori_loop(0, rows, first_dots, ((zero, zero), zero, zero, zero))
        keep_ends(kq, ends)
        if o == 0:
            pl.semaphore_wait(ready, nlat - 1)
        send_sums(k0, sums)
        send_halo(kq)
        observe()
        inside(q0, z0)
        wait_halo(kq)
        edges(q0, hq.at[kq], z0)

        def pack_z(row, ends):
            return pack_ends(row, z0[row + 1, 0], z0[row + 1, nblk - 1], ends)

        keep_ends(kz, lax.fori_loop(0, rows, pack_z, (zero, zero)))
        send_halo(kz)
        rr, rq, qq, _ = take_sums(k0)
        size0 = rr / rq
        beta0 = beta_of(size0, rr, rq, qq)
        more = 1.0 + beta0

        def second(row, carry):
            rr, rq, dq, qq = carry
            for cb in range(nblk):
                r, q, z = r0[row + 1, cb], q0[row + 1, cb], z0[row + 1, cb]
                res = r - size0 * q
                way = res + beta0 * r
                image = more * q - size0 * z
                r1[row + 1, cb] = res
                p1[row + 1, cb] = way
                q1[row + 1, cb] = image
                seen[row * nblk + cb] = image
                rr = rr + res * res
                rq = rq + res * image
                dq = dq + way * image
                qq = qq + image * image
            return rr, rq, dq, qq

        send_sums(kq, lax.fori_loop(0, rows, second, (zero,) * 4))
        observe()
        inside(q1, z1)
        wait_halo(kz)
        for edge in (0, rows + 1):
            for cb in range(nblk):
                q1[edge, cb] = more * q0[edge, cb] - size0 * z0[edge, cb]
        hq1[...] = more * hq[kq] - size0 * hq[kz]
        edges(q1, hq1, z1)
        rr, rq, dq, qq = take_sums(kq)
        size1 = rr / dq
        beta1 = beta_of(size1, rr, rq, qq)

        def third(row, carry):
            rr, dq = carry
            for cb in range(nblk):
                q = q1[row + 1, cb]
                res = r1[row + 1, cb] - size1 * q
                way = res + beta1 * p1[row + 1, cb]
                image = ((q0[row + 1, cb] - size0 * z0[row + 1, cb]) - size1 * z1[row + 1, cb]) + beta1 * q
                r2[row + 1, cb] = res
                p2[row + 1, cb] = way
                q2[row + 1, cb] = image
                rr = rr + res * res
                dq = dq + way * image
            return rr, dq

        send_sums(kz, lax.fori_loop(0, rows, third, (zero,) * 2))
        return size0, beta0, size1, beta1

    size0, beta0, size1, beta1 = outer(0)
    for c in obs_sends + first_copies:
        c.wait_send()

    def advance(row, carry):
        for cb in range(nblk):
            x[row + 1, cb] = size0 * field[0, row + 1, cb] + size1 * p1[row + 1, cb]
        return carry

    lax.fori_loop(0, rows, advance, 0)

    def beyond(r, q, q_next):
        res = r - size0 * q
        way = res + beta0 * r
        return size0 * r + size1 * way, (res - size1 * q_next) + beta1 * way

    for cb in range(nblk):
        x[rows + 1, cb], p2[rows + 1, cb] = beyond(field[0, rows + 1, cb], field[1, rows + 1, cb], q1[rows + 1, cb])
    hx[...], hp[...] = beyond(hq[0], hq[1], hq1[...])
    rr, dq, _, _ = take_sums(2)
    size2 = rr / dq

    def finish(row, carry):
        for cb in range(nblk):
            x[row + 1, cb] = x[row + 1, cb] + size2 * p2[row + 1, cb]
        return carry

    lax.fori_loop(0, rows + 1, finish, 0)
    hx[...] = hx[...] + size2 * hp[...]

    def friction(row, ends):
        v = [x[row + 1, cb] for cb in range(nblk)]
        e = eastward(v, from_east(hx, row))
        new = []
        for cb in range(nblk):
            at = pl.ds(cb * BLOCK, BLOCK)
            flux_e = coef[0, row, :, at] * (e[cb] - v[cb])
            flux_n = coef[2, row, :, at] * (x[row + 2, cb] - v[cb])
            square = flux_e * flux_e + flux_n * flux_n
            speed = jnp.sum(square[0] + square[1], axis=0, keepdims=True)
            extra = wetfric[row, :, at] * (jnp.sqrt(1.0 + speed / 16.0) - 1.0)
            diag[row, :, at] = diag[row, :, at] + extra
            new.append((r2[row + 1, cb] - size2 * q2[row + 1, cb]) - extra * v[cb])
            field[3, row + 1, cb] = new[cb]
            seen[row * nblk + cb] = new[cb]
        return pack_ends(row, new[0], new[-1], ends)

    keep_ends(3, lax.fori_loop(0, rows, friction, (zero, zero)))
    send_halo(3)
    size0, beta0, size1, beta1 = outer(1)

    def advance_last(row, carry):
        for cb in range(nblk):
            x[row + 1, cb] = (x[row + 1, cb] + size0 * field[3, row + 1, cb]) + size1 * p1[row + 1, cb]
        return carry

    lax.fori_loop(0, rows, advance_last, 0)
    outs = []
    for n, (src, dst) in enumerate(((x, x_out), (p2, p_out), (r2, r_out), (q2, q_out))):
        for cb in range(nblk):
            for h in range(2):
                turned[n, h, :, :, pl.ds(cb * BLOCK, BLOCK)] = jnp.swapaxes(src[pl.ds(1, rows), cb, h], 0, 1)
        outs.append(pltpu.make_async_copy(turned.at[n], dst, out_sem.at[n]))
        outs[n].start()
    for k in range(SUMS):
        for c in halo(k):
            c.wait_send()
    rr, dq, _, _ = take_sums(SUMS - 1)
    size_out[...] = jnp.broadcast_to((rr / dq)[:, 0:1], (8, cols))
    for i in range(SUMS):
        sum_wait(i).wait_send()
    for c in outs:
        c.wait()


def shards(nlat, nlon, depth, friction, ocean_mask, forcing, tile_route, tile_block, obs_cell, obs_time, obs_value, obs_weight):
    channels, rows, cols = forcing.shape
    slots = nlon * CAP
    nblk, tiles = cols // BLOCK, obs_time.shape[0]
    f32, i32 = jnp.float32, jnp.int32
    vmem, smem = pltpu.VMEM, pltpu.SMEM
    hbm = pl.BlockSpec(memory_space=pltpu.HBM)
    field = (rows + 2, nblk, 2, 8, BLOCK)
    ends = (2, 2, 8, BLOCK)
    split = (2, channels // 2, rows, cols)
    dma = pltpu.SemaphoreType.DMA
    scratch = [
        smem((tiles,), i32),
        smem((tiles,), i32),
        vmem((rows, cols), f32),
        vmem((rows, cols), f32),
        vmem((rows, cols), i32),
        vmem(split, f32),
        vmem((tiles, BLOCK), i32),
        vmem((tiles, BLOCK), f32),
        vmem((tiles, BLOCK), f32),
        vmem((tiles, BLOCK), f32),
        vmem((rows, cols), f32),
        vmem((rows, cols), f32),
        vmem((rows, cols), f32),
        vmem((rows, BLOCK), f32),
        vmem((rows, BLOCK), f32),
        vmem((rows, 8, cols), f32),
        vmem((4, rows, 8, cols), f32),
        vmem((rows, 8, cols), f32),
        vmem((tiles + 1, 8, BLOCK), f32),
        vmem((tiles + 1, 8, BLOCK), i32),
        vmem((nlon, 8, BLOCK), f32),
        vmem((nlon, 8, BLOCK), i32),
        vmem((nlon, 8, BLOCK), f32),
        vmem((nlon, 8, BLOCK), i32),
        vmem((8, BLOCK), i32),
        smem((8, BLOCK), i32),
        vmem((slots, 2, 8, BLOCK), f32),
        vmem((slots + 1, 256, BLOCK), f32),
        vmem((slots + 1, 2, 8, BLOCK), f32),
        vmem((SUMS,) + field, f32),
        vmem((rows * nblk, 2, 8, BLOCK), f32),
        vmem(field, f32),
        vmem(field, f32),
        vmem(field, f32),
        vmem(field, f32),
        vmem(field, f32),
        vmem(field, f32),
        vmem(field, f32),
        vmem(field, f32),
        vmem((4,) + split, f32),
        vmem((SUMS,) + ends, f32),
        vmem((SUMS,) + ends, f32),
        vmem(ends, f32),
        vmem(ends, f32),
        vmem(ends, f32),
        vmem((SUMS, nlat * nlon, BLOCK), f32),
        vmem((SUMS, 1, BLOCK), f32),
        pltpu.SemaphoreType.REGULAR,
        dma((10,)),
        dma((SUMS, 4)),
        dma((SUMS, 4)),
        dma((SUMS,)),
        dma((SUMS,)),
        dma((2, nlon)),
        dma((2, nlon)),
        dma((4,)),
        dma((4,)),
        dma((1,)),
        dma((4,)),
    ]
    shape = jax.ShapeDtypeStruct(split, f32)
    x, p, r, q, size = pl.pallas_call(
        functools.partial(kernel, nlat, nlon),
        out_shape=(shape, shape, shape, shape, jax.ShapeDtypeStruct((8, cols), f32)),
        in_specs=[hbm] * 10,
        out_specs=(hbm, hbm, hbm, hbm, pl.BlockSpec(memory_space=vmem)),
        scratch_shapes=scratch,
        compiler_params=pltpu.CompilerParams(
            collective_id=0, has_side_effects=True, vmem_limit_bytes=62 * 2**20
        ),
    )(
        tile_route.reshape(-1), tile_block, depth, friction, ocean_mask, forcing.reshape(split),
        obs_cell, obs_time, obs_value, obs_weight,
    )
    x, p, r, q = (v.reshape(forcing.shape) for v in (x, p, r, q))
    return x + size[0, 0] * p, r - size[0, 0] * q


def solution(mesh):
    tile = P(("lat", "lon"), None)
    grid = P("lat", "lon")
    in_specs = (grid, grid, grid, P(None, "lat", "lon"), tile, P(("lat", "lon")), tile, tile, tile, tile)
    out_specs = (P(None, "lat", "lon"), P(None, "lat", "lon"))
    body = functools.partial(shards, mesh.shape["lat"], mesh.shape["lon"])
    return jax.shard_map(body, mesh=mesh, in_specs=in_specs, out_specs=out_specs, check_vma=False)
```

time: 69.6 us -> 61.5 us (0.88)
  Pallas kernels: 66.1 us -> 56.1 us
  other arithmetic: 0 us -> 3.32 us
  local copies, waits for them, and re-layouts: 2.74 us -> 1.25 us
    pallas_call x1, Pallas kernels: 66.1 us -> 56.1 us  [shards(): pl.pallas_call(functools.partial(kernel, nlat, nlon), out_shape=(shape, s...]
    sub x0 -> x1, other arithmetic: none -> 3.32 us  [shards(): return (x + size[0, 0] * p, r - size[0, 0] * q)]
    unnamed x4 -> x0, local copies, waits for them, and re-layouts: 2.74 us -> none
    slice x0 -> x1, local copies, waits for them, and re-layouts: none -> 1.25 us  [shards(): return (x + size[0, 0] * p, r - size[0, 0] * q)]
where the time goes in v1:
time: 61.5 us; the launch traced here: 61.3 us
  Pallas kernels  56.1 us (91%)
  other arithmetic  3.32 us (5%)
  local copies, waits for them, and re-layouts  1.25 us (2%)
  between operations  0.64 us (1%)
    pallas_call x1, Pallas kernels, shards(): pl.pallas_call(functools.partial(kernel, nlat, nlon), out_shape=(shape, s...  56.1 us
    sub x1, other arithmetic, shards(): return (x + size[0, 0] * p, r - size[0, 0] * q)  3.32 us
    slice x1, local copies, waits for them, and re-layouts, shards(): return (x + size[0, 0] * p, r - size[0, 0] * q)  1.25 us

profile of v1, /device:TPU:0, one launch (start us, length us, event | category | flops | bytes accessed | tf_op | source)
XLA Modules:
  0.0 61.3 jit_solution(651013216396315327)
XLA Ops:
  0.6 56.1 %shard_map.113 = (f32[2,8,8,1024]{3,2,1,0:T(8,128)}, f32[2,8,8,1024]{3,2,1,0:T(8,128)}, f32[2,8,8,1024]{3,2,1,0:T(8,128)}, f32[2,8,8,1024]{3,2,1,0:T(8,128)}, f32[8,1024]{1,0:T(8,128)}) custom-call(s32[16]{0:T(128)} %bitcast.8, s32[16]{0:T(128)} %tblk_in.1, f32[8,1024]{1,0:T(8,128)} %depth_in.1, f32[8,1024]{1,0:T(8,128)} %fric_in.1, s32[8,1024]{1,0:T(8,128)} %mask_in.1, ...), custom_call_target="tpu_custom_call" | custom-call | tf_op jit(solution)/shard_map/pallas_call | solution.py:633
  56.7 1.2 %slice.4 = f32[1,1]{1,0:T(1,128)} slice(f32[8,1024]{1,0:T(8,128)} %get-tuple-element.8), slice={[0:1], [0:1]} | slice | bytes 8 | tf_op jit(solution)/shard_map/slice | solution.py:647
  58.0 3.3 %multiply_subtract_fusion = (f32[2,8,8,1024]{3,2,1,0:T(8,128)}, f32[2,8,8,1024]{3,2,1,0:T(8,128)}) fusion(f32[2,8,8,1024]{3,2,1,0:T(8,128)} %get-tuple-element.10, f32[2,8,8,1024]{3,2,1,0:T(8,128)} %get-tuple-element.11, f32[]{:T(128)} %bitcast.2, f32[2,8,8,1024]{3,2,1,0:T(8,128)} %get-tuple-element.7, f32[2,8,8,1024]{3,2,1,0:T(8,128)} %get-tuple-element.9), kind=kLoop, calls=%fused_computation | loop fusion | flops 524288 | bytes 3145732 | tf_op jit(solution)/shard_map/sub | solution.py:647

commit v2 on v1

--- a/solution.py
+++ b/solution.py
@@ -38,13 +38,13 @@
 def kernel(
     nlat, nlon,
     route_in, tblk_in, depth_in, fric_in, mask_in, forc_in, ocell_in, otime_in, oval_in, oweight_in,
-    x_out, p_out, r_out, q_out, size_out,
+    x_out, r_out,
     route, tblk, depth, fric, mask, forc, ocell, otime, oval, oweight,
     dw, dwn, dws, dwe, dww, wetfric, coef, diag,
     pay, payi, outf, outi, inf, ini, plan, splan, waves, mats, oslot,
     field, seen, r1, p1, q1, z1, r2, p2, q2, x, turned,
     pk, hq, hq1, hx, hp, sum_a, part_row, ready,
-    load, hs, hrv, as_, ar, os_, orv, ds_, dr, loc, out_sem,
+    load, hs, hrv, as_, ar, os_, orv, ds_, dr, loc,
 ):
     rows, cols = depth.shape
     nblk = cols // BLOCK
@@ -539,22 +539,27 @@
         return carry
 
     lax.fori_loop(0, rows, advance_last, 0)
-    outs = []
-    for n, (src, dst) in enumerate(((x, x_out), (p2, p_out), (r2, r_out), (q2, q_out))):
+    for n, src in enumerate((x, p2, r2, q2)):
         for cb in range(nblk):
             for h in range(2):
                 turned[n, h, :, :, pl.ds(cb * BLOCK, BLOCK)] = jnp.swapaxes(src[pl.ds(1, rows), cb, h], 0, 1)
-        outs.append(pltpu.make_async_copy(turned.at[n], dst, out_sem.at[n]))
-        outs[n].start()
     for k in range(SUMS):
         for c in halo(k):
             c.wait_send()
     rr, dq, _, _ = take_sums(SUMS - 1)
-    size_out[...] = jnp.broadcast_to((rr / dq)[:, 0:1], (8, cols))
+    size2 = rr / dq
+
+    def conclude(c, carry):
+        for h in range(2):
+            for cb in range(nblk):
+                at = pl.ds(cb * BLOCK, BLOCK)
+                x_out[h, c, :, at] = turned[0, h, c, :, at] + size2 * turned[1, h, c, :, at]
+                r_out[h, c, :, at] = turned[2, h, c, :, at] - size2 * turned[3, h, c, :, at]
+        return carry
+
+    lax.fori_loop(0, 8, conclude, 0)
     for i in range(SUMS):
         sum_wait(i).wait_send()
-    for c in outs:
-        c.wait()
 
 
 def shards(nlat, nlon, depth, friction, ocean_mask, forcing, tile_route, tile_block, obs_cell, obs_time, obs_value, obs_weight):
@@ -627,14 +632,13 @@
         dma((4,)),
         dma((4,)),
         dma((1,)),
-        dma((4,)),
     ]
-    shape = jax.ShapeDtypeStruct(split, f32)
-    x, p, r, q, size = pl.pallas_call(
+    shape = vmem(split, f32)
+    x, r = pl.pallas_call(
         functools.partial(kernel, nlat, nlon),
-        out_shape=(shape, shape, shape, shape, jax.ShapeDtypeStruct((8, cols), f32)),
+        out_shape=(shape, shape),
         in_specs=[hbm] * 10,
-        out_specs=(hbm, hbm, hbm, hbm, pl.BlockSpec(memory_space=vmem)),
+        out_specs=(pl.BlockSpec(memory_space=vmem), pl.BlockSpec(memory_space=vmem)),
         scratch_shapes=scratch,
         compiler_params=pltpu.CompilerParams(
             collective_id=0, has_side_effects=True, vmem_limit_bytes=62 * 2**20
@@ -643,8 +647,7 @@
         tile_route.reshape(-1), tile_block, depth, friction, ocean_mask, forcing.reshape(split),
         obs_cell, obs_time, obs_value, obs_weight,
     )
-    x, p, r, q = (v.reshape(forcing.shape) for v in (x, p, r, q))
-    return x + size[0, 0] * p, r - size[0, 0] * q
+    return x.reshape(forcing.shape), r.reshape(forcing.shape)
 
 
 def solution(mesh):

time: 61.5 us -> 57.9 us (0.941)
  other arithmetic: 3.32 us -> 0 us
    sub x1 -> x0, other arithmetic: 3.32 us -> none  [shards(): return (x + size[0, 0] * p, r - size[0, 0] * q)]
    unnamed x0 -> x2, local copies, waits for them, and re-layouts: none -> 1.59 us
    slice x1 -> x0, local copies, waits for them, and re-layouts: 1.25 us -> none  [shards(): return (x + size[0, 0] * p, r - size[0, 0] * q)]
where the time goes in v2:
time: 57.9 us; the launch traced here: 57.8 us
  Pallas kernels  55.5 us (96%)
  local copies, waits for them, and re-layouts  1.59 us (3%)
  between operations  0.64 us (1%)
    pallas_call x1, Pallas kernels, shards(): pl.pallas_call(functools.partial(kernel, nlat, nlon), out_shape=(shape, s...  55.5 us
    unnamed x2, local copies, waits for them, and re-layouts  1.59 us

profile of v2, /device:TPU:0, one launch (start us, length us, event | category | flops | bytes accessed | tf_op | source)
XLA Modules:
  0.0 57.8 jit_solution(2886515432527169642)
XLA Ops:
  0.6 55.5 %shard_map.113 = (f32[2,8,8,1024]{3,2,1,0:T(8,128)S(1)}, f32[2,8,8,1024]{3,2,1,0:T(8,128)S(1)}) custom-call(s32[16]{0:T(128)} %bitcast.7, s32[16]{0:T(128)} %tblk_in.1, f32[8,1024]{1,0:T(8,128)} %depth_in.1, f32[8,1024]{1,0:T(8,128)} %fric_in.1, s32[8,1024]{1,0:T(8,128)} %mask_in.1, f32[2,8,8,1024]{3,2,1,0:T(8,128)} %bitcast.6, s32[16,128]{1,0:T(8,128)} %ocell_in.1, ...), custom_call_target="tpu_custom_call" | custom-call | tf_op jit(solution)/shard_map/pallas_call | solution.py:637
  56.2 0.8 %copy.14 = f32[16,8,1024]{2,1,0:T(8,128)} copy(f32[16,8,1024]{2,1,0:T(8,128)S(1)} %bitcast.5) | data formatting | bytes 1048576
  57.0 0.8 %copy.15 = f32[16,8,1024]{2,1,0:T(8,128)} copy(f32[16,8,1024]{2,1,0:T(8,128)S(1)} %bitcast.4) | data formatting | bytes 1048576

commit v3 on v2

--- a/solution.py
+++ b/solution.py
@@ -14,6 +14,7 @@
 ITERS = 3
 OUTER = 2
 SUMS = ITERS * OUTER
+HALOS = 7
 MESH = pl.DeviceIdType.MESH
 OMEGA_DEGREES = (28.984104, 30.0, 28.43973, 30.082137, 15.041069, 13.943036, 14.958931, 13.398661)
 RATES = np.array(OMEGA_DEGREES, np.float32) * np.float32(math.pi / 180.0)
@@ -42,9 +43,9 @@
     route, tblk, depth, fric, mask, forc, ocell, otime, oval, oweight,
     dw, dwn, dws, dwe, dww, wetfric, coef, diag,
     pay, payi, outf, outi, inf, ini, plan, splan, waves, mats, oslot,
-    field, seen, r1, p1, q1, z1, r2, p2, q2, x, turned,
-    pk, hq, hq1, hx, hp, sum_a, part_row, ready,
-    load, hs, hrv, as_, ar, os_, orv, ds_, dr, loc,
+    field, seen, r1, p1, q1, z_last, r2, p2, q2, x, turned,
+    pk, hq, hq1, hx, hp, hr, hw, surf, surf_pk, surf_hq, sum_a, part_row, ready,
+    load, hs, hrv, ss, sr, as_, ar, os_, orv, ds_, dr, loc,
 ):
     rows, cols = depth.shape
     nblk = cols // BLOCK
@@ -324,31 +325,44 @@
     def from_west(halos, row):
         return pltpu.roll(halos[0], BLOCK - row, 2)
 
-    def image_row(src, dst, row, east_side, west_side):
+    def image_row(src, row, east_side, west_side, to_north=True, to_south=True):
         v = [src[row + 1, cb] for cb in range(nblk)]
         e = eastward(v, east_side)
         w = westward(v, west_side)
+        images = []
         for cb in range(nblk):
             at = pl.ds(cb * BLOCK, BLOCK)
-            dst[row + 1, cb] = (
+            image = (
                 diag[row, :, at] * v[cb]
                 - coef[0, row, :, at] * e[cb]
                 - coef[1, row, :, at] * w[cb]
-                - coef[2, row, :, at] * src[row + 2, cb]
-                - coef[3, row, :, at] * src[row, cb]
                 + oslot[splan[2, row * nblk + cb]]
             )
+            if to_north:
+                image = image - coef[2, row, :, at] * src[row + 2, cb]
+            if to_south:
+                image = image - coef[3, row, :, at] * src[row, cb]
+            images.append(image)
+        return v, images
 
     def inside(src, dst):
+        def put(row, images):
+            for cb in range(nblk):
+                dst[row + 1, cb] = images[cb]
+
         def line(row, carry):
-            image_row(src, dst, row, zero, zero)
+            put(row, image_row(src, row, zero, zero)[1])
             return carry
 
         lax.fori_loop(1, rows - 1, line, 0)
+        put(0, image_row(src, 0, zero, zero, to_south=False)[1])
+        put(rows - 1, image_row(src, rows - 1, zero, zero, to_north=False)[1])
 
     def edges(src, halos, dst):
-        for row in (0, rows - 1):
-            image_row(src, dst, row, from_east(halos, row), from_west(halos, row))
+        for cb in range(nblk):
+            at = pl.ds(cb * BLOCK, BLOCK)
+            dst[1, cb] = dst[1, cb] - coef[3, 0, :, at] * src[0, cb]
+            dst[rows, cb] = dst[rows, cb] - coef[2, rows - 1, :, at] * src[rows + 1, cb]
 
         def mend(row, carry):
             last = pl.ds(cols - BLOCK, BLOCK)
@@ -360,7 +374,7 @@
             )
             return carry
 
-        lax.fori_loop(1, rows - 1, mend, 0)
+        lax.fori_loop(0, rows, mend, 0)
 
     def sum_copy(i, k):
         peer = lax.rem(me + k, count)
@@ -396,41 +410,60 @@
     def beta_of(size, rr, rq, qq):
         return (rr - 2.0 * size * rq + size * size * qq) / rr
 
+    def pack_field(src):
+        def line(row, ends):
+            return pack_ends(row, src[row + 1, 0], src[row + 1, nblk - 1], ends)
+
+        return lax.fori_loop(0, rows, line, (zero, zero))
+
     def outer(o):
-        k0, kq, kz = 3 * o, 3 * o + 1, 3 * o + 2
+        k0, kq, kz = 4 * o, 4 * o + 1, 4 * o + 2
+        i0, i1, i2 = ITERS * o, ITERS * o + 1, ITERS * o + 2
         r0, q0, z0 = field.at[k0], field.at[kq], field.at[kz]
+        z1 = field.at[3] if o == 0 else z_last
         observe()
-        inside(r0, q0)
-        wait_halo(k0)
-        edges(r0, hq.at[k0], q0)
+        if o == 0:
+            inside(r0, q0)
+            wait_halo(k0)
+            edges(r0, hq.at[k0], q0)
 
         def first_dots(row, carry):
             ends, rr, rq, qq = carry
+            if o == 0:
+                v = [r0[row + 1, cb] for cb in range(nblk)]
+                images = [q0[row + 1, cb] for cb in range(nblk)]
+            else:
+                v, images = image_row(r0, row, from_east(hq.at[k0], row), from_west(hq.at[k0], row))
             for cb in range(nblk):
-                res, image = r0[row + 1, cb], q0[row + 1, cb]
-                seen[row * nblk + cb] = image
+                res, image = v[cb], images[cb]
+                if o > 0:
+                    q0[row + 1, cb] = image
                 rr = rr + res * res
                 rq = rq + res * image
                 qq = qq + image * image
-            return pack_ends(row, q0[row + 1, 0], q0[row + 1, nblk - 1], ends), rr, rq, qq
+            return pack_ends(row, images[0], images[-1], ends), rr, rq, qq
 
         ends, *sums = lax.fori_loop(0, rows, first_dots, ((zero, zero), zero, zero, zero))
         keep_ends(kq, ends)
         if o == 0:
             pl.semaphore_wait(ready, nlat - 1)
-        send_sums(k0, sums)
+        send_sums(i0, sums)
         send_halo(kq)
+
+        def look(row, carry):
+            for cb in range(nblk):
+                seen[row * nblk + cb] = q0[row + 1, cb]
+            return carry
+
+        lax.fori_loop(0, rows, look, 0)
         observe()
         inside(q0, z0)
         wait_halo(kq)
         edges(q0, hq.at[kq], z0)
 
-        def pack_z(row, ends):
-            return pack_ends(row, z0[row + 1, 0], z0[row + 1, nblk - 1], ends)
-
-        keep_ends(kz, lax.fori_loop(0, rows, pack_z, (zero, zero)))
+        keep_ends(kz, pack_field(z0))
         send_halo(kz)
-        rr, rq, qq, _ = take_sums(k0)
+        rr, rq, qq, _ = take_sums(i0)
         size0 = rr / rq
         beta0 = beta_of(size0, rr, rq, qq)
         more = 1.0 + beta0
@@ -452,7 +485,7 @@
                 qq = qq + image * image
             return rr, rq, dq, qq
 
-        send_sums(kq, lax.fori_loop(0, rows, second, (zero,) * 4))
+        send_sums(i1, lax.fori_loop(0, rows, second, (zero,) * 4))
         observe()
         inside(q1, z1)
         wait_halo(kz)
@@ -461,7 +494,10 @@
                 q1[edge, cb] = more * q0[edge, cb] - size0 * z0[edge, cb]
         hq1[...] = more * hq[kq] - size0 * hq[kz]
         edges(q1, hq1, z1)
-        rr, rq, dq, qq = take_sums(kq)
+        if o == 0:
+            keep_ends(3, pack_field(z1))
+            send_halo(3)
+        rr, rq, dq, qq = take_sums(i1)
         size1 = rr / dq
         beta1 = beta_of(size1, rr, rq, qq)
 
@@ -479,63 +515,123 @@
                 dq = dq + way * image
             return rr, dq
 
-        send_sums(kz, lax.fori_loop(0, rows, third, (zero,) * 2))
+        send_sums(i2, lax.fori_loop(0, rows, third, (zero,) * 2))
         return size0, beta0, size1, beta1
 
     size0, beta0, size1, beta1 = outer(0)
     for c in obs_sends + first_copies:
         c.wait_send()
 
-    def advance(row, carry):
-        for cb in range(nblk):
-            x[row + 1, cb] = size0 * field[0, row + 1, cb] + size1 * p1[row + 1, cb]
-        return carry
-
-    lax.fori_loop(0, rows, advance, 0)
-
     def beyond(r, q, q_next):
         res = r - size0 * q
         way = res + beta0 * r
-        return size0 * r + size1 * way, (res - size1 * q_next) + beta1 * way
-
-    for cb in range(nblk):
-        x[rows + 1, cb], p2[rows + 1, cb] = beyond(field[0, rows + 1, cb], field[1, rows + 1, cb], q1[rows + 1, cb])
-    hx[...], hp[...] = beyond(hq[0], hq[1], hq1[...])
+        res = res - size1 * q_next
+        return size0 * r + size1 * way, res + beta1 * way, res
+
+    for edge in (0, rows + 1):
+        for cb in range(nblk):
+            x[edge, cb], p2[edge, cb], r2[edge, cb] = beyond(field[0, edge, cb], field[1, edge, cb], q1[edge, cb])
+    hx[...], hp[...], hr[...] = beyond(hq[0], hq[1], hq1[...])
+
+    def advance(row, carry):
+        for cb in range(nblk):
+            x[row + 1, cb] = size0 * field[0, row + 1, cb] + size1 * p1[row + 1, cb]
+        return carry
+
+    lax.fori_loop(0, rows, advance, 0)
+
+    def add_up(square):
+        return jnp.sum(square[0] + square[1], axis=0, keepdims=True)
+
+    def surface(row, cb):
+        at = pl.ds(cb * BLOCK, BLOCK)
+        flux = []
+        for ref, halos in ((x, hx), (p2, hp)):
+            v = ref[row + 1, cb]
+            after = pltpu.roll(ref[row + 1, cb + 1], BLOCK - 1, 2) if cb < nblk - 1 else from_east(halos, row)
+            e = jnp.where(lane8 == BLOCK - 1, after, pltpu.roll(v, BLOCK - 1, 2))
+            flux.append((coef[0, row, :, at] * (e - v), coef[2, row, :, at] * (ref[row + 2, cb] - v)))
+        (xe, xn), (pe, pn) = flux
+        parts = jnp.where(sub8 == 0, add_up(xe * xe + xn * xn), wetfric[row, :, at])
+        parts = jnp.where(sub8 == 1, add_up(xe * pe + xn * pn), parts)
+        parts = jnp.where(sub8 == 2, add_up(pe * pe + pn * pn), parts)
+        surf[row + 1, :, at] = parts
+        return parts
+
+    def surface_ends(row, ends):
+        first, last = surface(row, 0), surface(row, nblk - 1)
+        return (
+            jnp.where(lane8 == row, pltpu.roll(first, row, 1), ends[0]),
+            jnp.where(lane8 == row, pltpu.roll(last, row + 1, 1), ends[1]),
+        )
+
+    blank = jnp.zeros((8, BLOCK), jnp.float32)
+    ends = lax.fori_loop(0, rows, surface_ends, (blank, blank))
+    surf_pk[0] = ends[0]
+    surf_pk[1] = ends[1]
+    surf_copies = [
+        remote(surf_pk.at[0], surf_hq.at[1], ss.at[2], sr.at[2], {"lon": west}),
+        remote(surf_pk.at[1], surf_hq.at[0], ss.at[3], sr.at[3], {"lon": east}),
+        remote(surf.at[1], surf.at[rows + 1], ss.at[0], sr.at[0], {"lat": south}),
+        remote(surf.at[rows], surf.at[0], ss.at[1], sr.at[1], {"lat": north}),
+    ]
+    for c in surf_copies[:2]:
+        c.start()
+
+    def surface_middle(row, carry):
+        for cb in range(1, nblk - 1):
+            surface(row, cb)
+        return carry
+
+    lax.fori_loop(0, rows, surface_middle, 0)
+    for c in surf_copies[2:]:
+        c.start()
+    wait_halo(3)
+
+    def image_beyond(q, z, z_next, q_next):
+        return ((q - size0 * z) - size1 * z_next) + beta1 * q_next
+
+    for edge in (0, rows + 1):
+        for cb in range(nblk):
+            q2[edge, cb] = image_beyond(field[1, edge, cb], field[2, edge, cb], field[3, edge, cb], q1[edge, cb])
+    hw[...] = image_beyond(hq[1], hq[2], hq[3], hq1[...])
+    for c in surf_copies:
+        c.wait_recv()
     rr, dq, _, _ = take_sums(2)
     size2 = rr / dq
-
-    def finish(row, carry):
-        for cb in range(nblk):
-            x[row + 1, cb] = x[row + 1, cb] + size2 * p2[row + 1, cb]
-        return carry
-
-    lax.fori_loop(0, rows + 1, finish, 0)
-    hx[...] = hx[...] + size2 * hp[...]
-
-    def friction(row, ends):
-        v = [x[row + 1, cb] for cb in range(nblk)]
-        e = eastward(v, from_east(hx, row))
-        new = []
+    ramp = jnp.where(sub8 == 0, 1.0, jnp.where(sub8 == 1, 2.0 * size2, jnp.where(sub8 == 2, size2 * size2, 0.0)))
+
+    def extra_of(parts):
+        speed = jnp.maximum(jnp.sum(parts * ramp, axis=0, keepdims=True), 0.0)
+        return parts[3:4] * (jnp.sqrt(1.0 + speed / 16.0) - 1.0)
+
+    def renew(row, cb):
+        extra = extra_of(surf[row, :, pl.ds(cb * BLOCK, BLOCK)])
+        place = x[row, cb] + size2 * p2[row, cb]
+        new = (r2[row, cb] - size2 * q2[row, cb]) - extra * place
+        field[4, row, cb] = new
+        return extra, place, new
+
+    def friction(row, carry):
         for cb in range(nblk):
             at = pl.ds(cb * BLOCK, BLOCK)
-            flux_e = coef[0, row, :, at] * (e[cb] - v[cb])
-            flux_n = coef[2, row, :, at] * (x[row + 2, cb] - v[cb])
-            square = flux_e * flux_e + flux_n * flux_n
-            speed = jnp.sum(square[0] + square[1], axis=0, keepdims=True)
-            extra = wetfric[row, :, at] * (jnp.sqrt(1.0 + speed / 16.0) - 1.0)
+            extra, place, new = renew(row + 1, cb)
+            x[row + 1, cb] = place
             diag[row, :, at] = diag[row, :, at] + extra
-            new.append((r2[row + 1, cb] - size2 * q2[row + 1, cb]) - extra * v[cb])
-            field[3, row + 1, cb] = new[cb]
-            seen[row * nblk + cb] = new[cb]
-        return pack_ends(row, new[0], new[-1], ends)
-
-    keep_ends(3, lax.fori_loop(0, rows, friction, (zero, zero)))
-    send_halo(3)
+            seen[row * nblk + cb] = new
+        return carry
+
+    lax.fori_loop(0, rows, friction, 0)
+    for edge in (0, rows + 1):
+        for cb in range(nblk):
+            renew(edge, cb)
+    for side in range(2):
+        hq[4, side] = (hr[side] - size2 * hw[side]) - extra_of(surf_hq[side]) * (hx[side] + size2 * hp[side])
     size0, beta0, size1, beta1 = outer(1)
 
     def advance_last(row, carry):
         for cb in range(nblk):
-            x[row + 1, cb] = (x[row + 1, cb] + size0 * field[3, row + 1, cb]) + size1 * p1[row + 1, cb]
+            x[row + 1, cb] = (x[row + 1, cb] + size0 * field[4, row + 1, cb]) + size1 * p1[row + 1, cb]
         return carry
 
     lax.fori_loop(0, rows, advance_last, 0)
@@ -543,9 +639,11 @@
         for cb in range(nblk):
             for h in range(2):
                 turned[n, h, :, :, pl.ds(cb * BLOCK, BLOCK)] = jnp.swapaxes(src[pl.ds(1, rows), cb, h], 0, 1)
-    for k in range(SUMS):
+    for k in (0, 1, 2, 3, 5, 6):
         for c in halo(k):
             c.wait_send()
+    for c in surf_copies:
+        c.wait_send()
     rr, dq, _, _ = take_sums(SUMS - 1)
     size2 = rr / dq
 
@@ -603,7 +701,7 @@
         vmem((slots, 2, 8, BLOCK), f32),
         vmem((slots + 1, 256, BLOCK), f32),
         vmem((slots + 1, 2, 8, BLOCK), f32),
-        vmem((SUMS,) + field, f32),
+        vmem((HALOS,) + field, f32),
         vmem((rows * nblk, 2, 8, BLOCK), f32),
         vmem(field, f32),
         vmem(field, f32),
@@ -614,17 +712,24 @@
         vmem(field, f32),
         vmem(field, f32),
         vmem((4,) + split, f32),
-        vmem((SUMS,) + ends, f32),
-        vmem((SUMS,) + ends, f32),
+        vmem((HALOS,) + ends, f32),
+        vmem((HALOS,) + ends, f32),
         vmem(ends, f32),
         vmem(ends, f32),
         vmem(ends, f32),
+        vmem(ends, f32),
+        vmem(ends, f32),
+        vmem((rows + 2, 8, cols), f32),
+        vmem((2, 8, BLOCK), f32),
+        vmem((2, 8, BLOCK), f32),
         vmem((SUMS, nlat * nlon, BLOCK), f32),
         vmem((SUMS, 1, BLOCK), f32),
         pltpu.SemaphoreType.REGULAR,
         dma((10,)),
-        dma((SUMS, 4)),
-        dma((SUMS, 4)),
+        dma((HALOS, 4)),
+        dma((HALOS, 4)),
+        dma((4,)),
+        dma((4,)),
         dma((SUMS,)),
         dma((SUMS,)),
         dma((2, nlon)),

time: 57.9 us -> 55.4 us (0.957)
  Pallas kernels: 55.5 us -> 53 us
    pallas_call x1, Pallas kernels: 55.5 us -> 53 us  [shards(): pl.pallas_call(functools.partial(kernel, nlat, nlon), out_shape=(shape, s...]
where the time goes in v3:
time: 55.4 us; the launch traced here: 55.3 us
  Pallas kernels  53 us (96%)
  local copies, waits for them, and re-layouts  1.59 us (3%)
  between operations  0.64 us (1%)
    pallas_call x1, Pallas kernels, shards(): pl.pallas_call(functools.partial(kernel, nlat, nlon), out_shape=(shape, s...  53 us
    unnamed x2, local copies, waits for them, and re-layouts  1.59 us

profile of v3, /device:TPU:0, one launch (start us, length us, event | category | flops | bytes accessed | tf_op | source)
XLA Modules:
  0.0 55.3 jit_solution(3627596912945523585)
XLA Ops:
  0.6 53.0 %shard_map.113 = (f32[2,8,8,1024]{3,2,1,0:T(8,128)S(1)}, f32[2,8,8,1024]{3,2,1,0:T(8,128)S(1)}) custom-call(s32[16]{0:T(128)} %bitcast.7, s32[16]{0:T(128)} %tblk_in.1, f32[8,1024]{1,0:T(8,128)} %depth_in.1, f32[8,1024]{1,0:T(8,128)} %fric_in.1, s32[8,1024]{1,0:T(8,128)} %mask_in.1, f32[2,8,8,1024]{3,2,1,0:T(8,128)} %bitcast.6, s32[16,128]{1,0:T(8,128)} %ocell_in.1, ...), custom_call_target="tpu_custom_call" | custom-call | tf_op jit(solution)/shard_map/pallas_call | solution.py:742
  53.7 0.8 %copy.14 = f32[16,8,1024]{2,1,0:T(8,128)} copy(f32[16,8,1024]{2,1,0:T(8,128)S(1)} %bitcast.5) | data formatting | bytes 1048576
  54.5 0.8 %copy.15 = f32[16,8,1024]{2,1,0:T(8,128)} copy(f32[16,8,1024]{2,1,0:T(8,128)S(1)} %bitcast.4) | data formatting | bytes 1048576

commit v4 on v3

--- a/solution.py
+++ b/solution.py
@@ -207,27 +207,23 @@
 
     lax.fori_loop(0, slots, join_values, 0)
 
-    def pack(row, col, value, packed):
-        shift = row if col == 0 else row + 1
-        moved = pltpu.roll(value, shift, 2)
-        return jnp.where(lane8 == row, moved, packed)
-
-    def pack_ends(row, first, last, carry):
-        return pack(row, 0, first, carry[0]), pack(row, 1, last, carry[1])
-
-    def keep_ends(k, ends):
-        pk[k, 0] = ends[0]
-        pk[k, 1] = ends[1]
-
-    def start_rhs(row, ends):
-        v = []
-        for cb in range(nblk):
-            v.append(field[0, row + 1, cb] + oslot[splan[2, row * nblk + cb]])
-            field[0, row + 1, cb] = v[cb]
-            seen[row * nblk + cb] = v[cb]
-        return pack_ends(row, v[0], v[-1], ends)
-
-    keep_ends(0, lax.fori_loop(0, rows, start_rhs, (zero, zero)))
+    def keep_ends(k, src):
+        for side, cb in enumerate((0, nblk - 1)):
+            packed = zero
+            for row in range(rows):
+                moved = pltpu.roll(src[row + 1, cb], (row + side) % BLOCK, 2)
+                packed = jnp.where(lane8 == row, moved, packed)
+            pk[k, side] = packed
+
+    def start_rhs(row, carry):
+        for cb in range(nblk):
+            v = field[0, row + 1, cb] + oslot[splan[2, row * nblk + cb]]
+            field[0, row + 1, cb] = v
+            seen[row * nblk + cb] = v
+        return carry
+
+    lax.fori_loop(0, rows, start_rhs, 0, unroll=2)
+    keep_ends(0, field.at[0])
 
     def halo(k):
         return [
@@ -237,8 +233,8 @@
             remote(field.at[k, rows], field.at[k, 0], hs.at[k, 1], hrv.at[k, 1], {"lat": north}),
         ]
 
-    def send_halo(k):
-        for c in halo(k):
+    def send_halo(k, part=slice(None)):
+        for c in halo(k)[part]:
             c.start()
 
     def wait_halo(k):
@@ -354,7 +350,7 @@
             put(row, image_row(src, row, zero, zero)[1])
             return carry
 
-        lax.fori_loop(1, rows - 1, line, 0)
+        lax.fori_loop(1, rows - 1, line, 0, unroll=2)
         put(0, image_row(src, 0, zero, zero, to_south=False)[1])
         put(rows - 1, image_row(src, rows - 1, zero, zero, to_north=False)[1])
 
@@ -364,17 +360,12 @@
             dst[1, cb] = dst[1, cb] - coef[3, 0, :, at] * src[0, cb]
             dst[rows, cb] = dst[rows, cb] - coef[2, rows - 1, :, at] * src[rows + 1, cb]
 
-        def mend(row, carry):
-            last = pl.ds(cols - BLOCK, BLOCK)
-            dst[row + 1, 0] = dst[row + 1, 0] - coef[1, row, :, pl.ds(0, BLOCK)] * jnp.where(
-                lane8 == 0, from_west(halos, row), 0.0
-            )
-            dst[row + 1, nblk - 1] = dst[row + 1, nblk - 1] - coef[0, row, :, last] * jnp.where(
-                lane8 == BLOCK - 1, from_east(halos, row), 0.0
-            )
-            return carry
-
-        lax.fori_loop(0, rows, mend, 0)
+        first, last = pl.ds(0, BLOCK), pl.ds(cols - BLOCK, BLOCK)
+        for row in range(rows):
+            beside = jnp.where(lane8 == 0, from_west(halos, row), 0.0)
+            dst[row + 1, 0] = dst[row + 1, 0] - coef[1, row, :, first] * beside
+            beside = jnp.where(lane8 == BLOCK - 1, from_east(halos, row), 0.0)
+            dst[row + 1, nblk - 1] = dst[row + 1, nblk - 1] - coef[0, row, :, last] * beside
 
     def sum_copy(i, k):
         peer = lax.rem(me + k, count)
@@ -409,12 +400,6 @@
 
     def beta_of(size, rr, rq, qq):
         return (rr - 2.0 * size * rq + size * size * qq) / rr
-
-    def pack_field(src):
-        def line(row, ends):
-            return pack_ends(row, src[row + 1, 0], src[row + 1, nblk - 1], ends)
-
-        return lax.fori_loop(0, rows, line, (zero, zero))
 
     def outer(o):
         k0, kq, kz = 4 * o, 4 * o + 1, 4 * o + 2
@@ -428,7 +413,7 @@
             edges(r0, hq.at[k0], q0)
 
         def first_dots(row, carry):
-            ends, rr, rq, qq = carry
+            rr, rq, qq = carry
             if o == 0:
                 v = [r0[row + 1, cb] for cb in range(nblk)]
                 images = [q0[row + 1, cb] for cb in range(nblk)]
@@ -441,14 +426,15 @@
                 rr = rr + res * res
                 rq = rq + res * image
                 qq = qq + image * image
-            return pack_ends(row, images[0], images[-1], ends), rr, rq, qq
-
-        ends, *sums = lax.fori_loop(0, rows, first_dots, ((zero, zero), zero, zero, zero))
-        keep_ends(kq, ends)
+            return rr, rq, qq
+
+        sums = lax.fori_loop(0, rows, first_dots, (zero, zero, zero), unroll=2)
+        keep_ends(kq, q0)
+        send_halo(kq, slice(0, 2))
         if o == 0:
             pl.semaphore_wait(ready, nlat - 1)
         send_sums(i0, sums)
-        send_halo(kq)
+        send_halo(kq, slice(2, 4))
 
         def look(row, carry):
             for cb in range(nblk):
@@ -461,7 +447,7 @@
         wait_halo(kq)
         edges(q0, hq.at[kq], z0)
 
-        keep_ends(kz, pack_field(z0))
+        keep_ends(kz, z0)
         send_halo(kz)
         rr, rq, qq, _ = take_sums(i0)
         size0 = rr / rq
@@ -485,7 +471,7 @@
                 qq = qq + image * image
             return rr, rq, dq, qq
 
-        send_sums(i1, lax.fori_loop(0, rows, second, (zero,) * 4))
+        send_sums(i1, lax.fori_loop(0, rows, second, (zero,) * 4, unroll=2))
         observe()
         inside(q1, z1)
         wait_halo(kz)
@@ -495,7 +481,7 @@
         hq1[...] = more * hq[kq] - size0 * hq[kz]
         edges(q1, hq1, z1)
         if o == 0:
-            keep_ends(3, pack_field(z1))
+            keep_ends(3, z1)
             send_halo(3)
         rr, rq, dq, qq = take_sums(i1)
         size1 = rr / dq
@@ -515,7 +501,7 @@
                 dq = dq + way * image
             return rr, dq
 
-        send_sums(i2, lax.fori_loop(0, rows, third, (zero,) * 2))
+        send_sums(i2, lax.fori_loop(0, rows, third, (zero,) * 2, unroll=2))
         return size0, beta0, size1, beta1
 
     size0, beta0, size1, beta1 = outer(0)
@@ -621,7 +607,7 @@
             seen[row * nblk + cb] = new
         return carry
 
-    lax.fori_loop(0, rows, friction, 0)
+    lax.fori_loop(0, rows, friction, 0, unroll=2)
     for edge in (0, rows + 1):
         for cb in range(nblk):
             renew(edge, cb)

time: 55.4 us -> 51.5 us (0.930)
  Pallas kernels: 53 us -> 49.1 us
    pallas_call x1, Pallas kernels: 53 us -> 49.1 us  [shards(): pl.pallas_call(functools.partial(kernel, nlat, nlon), out_shape=(shape, s...]
where the time goes in v4:
time: 51.5 us; the launch traced here: 51.3 us
  Pallas kernels  49.1 us (95%)
  local copies, waits for them, and re-layouts  1.59 us (3%)
  between operations  0.64 us (1%)
    pallas_call x1, Pallas kernels, shards(): pl.pallas_call(functools.partial(kernel, nlat, nlon), out_shape=(shape, s...  49.1 us
    unnamed x2, local copies, waits for them, and re-layouts  1.59 us

profile of v4, /device:TPU:0, one launch (start us, length us, event | category | flops | bytes accessed | tf_op | source)
XLA Modules:
  0.0 51.3 jit_solution(5158018381538656955)
XLA Ops:
  0.6 49.1 %shard_map.113 = (f32[2,8,8,1024]{3,2,1,0:T(8,128)S(1)}, f32[2,8,8,1024]{3,2,1,0:T(8,128)S(1)}) custom-call(s32[16]{0:T(128)} %bitcast.7, s32[16]{0:T(128)} %tblk_in.1, f32[8,1024]{1,0:T(8,128)} %depth_in.1, f32[8,1024]{1,0:T(8,128)} %fric_in.1, s32[8,1024]{1,0:T(8,128)} %mask_in.1, f32[2,8,8,1024]{3,2,1,0:T(8,128)} %bitcast.6, s32[16,128]{1,0:T(8,128)} %ocell_in.1, ...), custom_call_target="tpu_custom_call" | custom-call | tf_op jit(solution)/shard_map/pallas_call | solution.py:728
  49.7 0.8 %copy.14 = f32[16,8,1024]{2,1,0:T(8,128)} copy(f32[16,8,1024]{2,1,0:T(8,128)S(1)} %bitcast.5) | data formatting | bytes 1048576
  50.5 0.8 %copy.15 = f32[16,8,1024]{2,1,0:T(8,128)} copy(f32[16,8,1024]{2,1,0:T(8,128)S(1)} %bitcast.4) | data formatting | bytes 1048576

commit v5 on v4

--- a/solution.py
+++ b/solution.py
@@ -39,11 +39,11 @@
 def kernel(
     nlat, nlon,
     route_in, tblk_in, depth_in, fric_in, mask_in, forc_in, ocell_in, otime_in, oval_in, oweight_in,
-    x_out, r_out,
+    x_out, p_out, r_out, q_out, size_out,
     route, tblk, depth, fric, mask, forc, ocell, otime, oval, oweight,
     dw, dwn, dws, dwe, dww, wetfric, coef, diag,
     pay, payi, outf, outi, inf, ini, plan, splan, waves, mats, oslot,
-    field, seen, r1, p1, q1, z_last, r2, p2, q2, x, turned,
+    field, seen, r1, p1, q1, z_last, r2, p2, q2, x,
     pk, hq, hq1, hx, hp, hr, hw, surf, surf_pk, surf_hq, sum_a, part_row, ready,
     load, hs, hrv, ss, sr, as_, ar, os_, orv, ds_, dr, loc,
 ):
@@ -215,14 +215,17 @@
                 packed = jnp.where(lane8 == row, moved, packed)
             pk[k, side] = packed
 
-    def start_rhs(row, carry):
-        for cb in range(nblk):
-            v = field[0, row + 1, cb] + oslot[splan[2, row * nblk + cb]]
-            field[0, row + 1, cb] = v
-            seen[row * nblk + cb] = v
-        return carry
-
-    lax.fori_loop(0, rows, start_rhs, 0, unroll=2)
+    def start_rhs(blocks):
+        def line(row, carry):
+            for cb in blocks:
+                v = field[0, row + 1, cb] + oslot[splan[2, row * nblk + cb]]
+                field[0, row + 1, cb] = v
+                seen[row * nblk + cb] = v
+            return carry
+
+        lax.fori_loop(0, rows, line, 0, unroll=rows if len(blocks) == 2 else 2)
+
+    start_rhs((0, nblk - 1))
     keep_ends(0, field.at[0])
 
     def halo(k):
@@ -241,7 +244,9 @@
         for c in halo(k):
             c.wait_recv()
 
-    send_halo(0)
+    send_halo(0, slice(0, 2))
+    start_rhs(range(1, nblk - 1))
+    send_halo(0, slice(2, 4))
 
     for c in first_copies:
         c.wait_recv()
@@ -367,10 +372,10 @@
             beside = jnp.where(lane8 == BLOCK - 1, from_east(halos, row), 0.0)
             dst[row + 1, nblk - 1] = dst[row + 1, nblk - 1] - coef[0, row, :, last] * beside
 
-    def sum_copy(i, k):
-        peer = lax.rem(me + k, count)
-        where = {"lat": peer // nlon, "lon": lax.rem(peer, nlon)}
-        return remote(part_row.at[i], sum_a.at[i, pl.ds(me, 1)], as_.at[i], ar.at[i], where)
+    lat_order = sorted(range(nlat), key=lambda k: (k == 0, abs(k - nlat // 2)))
+    lon_order = sorted(range(nlon), key=lambda k: (k == 0, k % 2 == 0, -abs(k - nlon // 2)))
+    lat_peers = {k: lax.rem(me_lat + k, nlat) for k in lat_order}
+    lon_peers = {k: lax.rem(me_lon + k, nlon) for k in lon_order}
 
     def sum_wait(i):
         whole = sum_a.at[i, pl.ds(0, count - 1)]
@@ -379,18 +384,18 @@
     def send_sums(i, sums):
         part = jnp.zeros((8, BLOCK), jnp.float32)
         for k, s in enumerate(sums):
-            part = jnp.where(sub8 == k, jnp.sum(s[0] + s[1], axis=0, keepdims=True), part)
-        part = part + pltpu.roll(part, 64, 1)
-        part = part + pltpu.roll(part, 32, 1)
-        row = jnp.sum(jnp.where(lane8 >> 5 == sub8, part, 0.0), axis=0, keepdims=True)
+            both = s[0] + s[1]
+            both = both + pltpu.roll(both, 64, 1)
+            both = both + pltpu.roll(both, 32, 1)
+            part = jnp.where(lane8 >> 5 == k, both, part)
+        row = jnp.sum(part, axis=0, keepdims=True)
         part_row[i] = row
         sum_a[i, pl.ds(me, 1)] = row
-
-        def send(k, carry):
-            sum_copy(i, k).start()
-            return carry
-
-        lax.fori_loop(1, count, send, 0, unroll=True)
+        for a in lat_order:
+            for b in lon_order:
+                if a or b:
+                    where = {"lat": lat_peers[a], "lon": lon_peers[b]}
+                    remote(part_row.at[i], sum_a.at[i, pl.ds(me, 1)], as_.at[i], ar.at[i], where).start()
 
     def take_sums(i):
         sum_wait(i).wait_recv()
@@ -621,27 +626,17 @@
         return carry
 
     lax.fori_loop(0, rows, advance_last, 0)
-    for n, src in enumerate((x, p2, r2, q2)):
+    for src, dst in ((x, x_out), (p2, p_out), (r2, r_out), (q2, q_out)):
         for cb in range(nblk):
             for h in range(2):
-                turned[n, h, :, :, pl.ds(cb * BLOCK, BLOCK)] = jnp.swapaxes(src[pl.ds(1, rows), cb, h], 0, 1)
+                dst[h, :, :, pl.ds(cb * BLOCK, BLOCK)] = jnp.swapaxes(src[pl.ds(1, rows), cb, h], 0, 1)
     for k in (0, 1, 2, 3, 5, 6):
         for c in halo(k):
             c.wait_send()
     for c in surf_copies:
         c.wait_send()
     rr, dq, _, _ = take_sums(SUMS - 1)
-    size2 = rr / dq
-
-    def conclude(c, carry):
-        for h in range(2):
-            for cb in range(nblk):
-                at = pl.ds(cb * BLOCK, BLOCK)
-                x_out[h, c, :, at] = turned[0, h, c, :, at] + size2 * turned[1, h, c, :, at]
-                r_out[h, c, :, at] = turned[2, h, c, :, at] - size2 * turned[3, h, c, :, at]
-        return carry
-
-    lax.fori_loop(0, 8, conclude, 0)
+    size_out[...] = jnp.broadcast_to((rr / dq)[:, 0:1], (8, cols))
     for i in range(SUMS):
         sum_wait(i).wait_send()
 
@@ -697,7 +692,6 @@
         vmem(field, f32),
         vmem(field, f32),
         vmem(field, f32),
-        vmem((4,) + split, f32),
         vmem((HALOS,) + ends, f32),
         vmem((HALOS,) + ends, f32),
         vmem(ends, f32),
@@ -725,20 +719,20 @@
         dma((1,)),
     ]
     shape = vmem(split, f32)
-    x, r = pl.pallas_call(
+    x, p, r, q, size = pl.pallas_call(
         functools.partial(kernel, nlat, nlon),
-        out_shape=(shape, shape),
+        out_shape=(shape,) * 4 + (vmem((rows, cols), f32),),
         in_specs=[hbm] * 10,
-        out_specs=(pl.BlockSpec(memory_space=vmem), pl.BlockSpec(memory_space=vmem)),
+        out_specs=(pl.BlockSpec(memory_space=vmem),) * 5,
         scratch_shapes=scratch,
         compiler_params=pltpu.CompilerParams(
-            collective_id=0, has_side_effects=True, vmem_limit_bytes=62 * 2**20
+            collective_id=0, has_side_effects=True, vmem_limit_bytes=61 * 2**20
         ),
     )(
         tile_route.reshape(-1), tile_block, depth, friction, ocean_mask, forcing.reshape(split),
         obs_cell, obs_time, obs_value, obs_weight,
     )
-    return x.reshape(forcing.shape), r.reshape(forcing.shape)
+    return (x + size * p).reshape(forcing.shape), (r - size * q).reshape(forcing.shape)
 
 
 def solution(mesh):

time: 51.5 us -> 50.5 us (0.981)
  local copies, waits for them, and re-layouts: 1.59 us -> 0 us
  other arithmetic: 0 us -> 1.19 us
  Pallas kernels: 49.1 us -> 48.5 us
    unnamed x2 -> x0, local copies, waits for them, and re-layouts: 1.59 us -> none
    sub x0 -> x1, other arithmetic: none -> 1.19 us  [shards(): r - size * q]
    pallas_call x1, Pallas kernels: 49.1 us -> 48.5 us  [shards(): pl.pallas_call(functools.partial(kernel, nlat, nlon), out_shape=(shape,)...]
where the time goes in v5:
time: 50.5 us; the launch traced here: 50.3 us
  Pallas kernels  48.5 us (96%)
  other arithmetic  1.19 us (2%)
  between operations  0.64 us (1%)
    pallas_call x1, Pallas kernels, shards(): pl.pallas_call(functools.partial(kernel, nlat, nlon), out_shape=(shape,)...  48.5 us
    sub x1, other arithmetic, shards(): r - size * q  1.19 us

profile of v5, /device:TPU:0, one launch (start us, length us, event | category | flops | bytes accessed | tf_op | source)
XLA Modules:
  0.0 50.3 jit_solution(585219467100170195)
XLA Ops:
  0.6 48.5 %shard_map.113 = (f32[2,8,8,1024]{3,2,1,0:T(8,128)S(1)}, f32[2,8,8,1024]{3,2,1,0:T(8,128)S(1)}, f32[2,8,8,1024]{3,2,1,0:T(8,128)S(1)}, f32[2,8,8,1024]{3,2,1,0:T(8,128)S(1)}, f32[8,1024]{1,0:T(8,128)S(1)}) custom-call(s32[16]{0:T(128)} %bitcast.7, s32[16]{0:T(128)} %tblk_in.1, f32[8,1024]{1,0:T(8,128)} %depth_in.1, f32[8,1024]{1,0:T(8,128)} %fric_in.1, ...), custom_call_target="tpu_custom_call" | custom-call | tf_op jit(solution)/shard_map/pallas_call | solution.py:722
  49.1 1.2 %multiply_subtract_fusion = (f32[2,8,8,1024]{3,2,1,0:T(8,128)}, f32[2,8,8,1024]{3,2,1,0:T(8,128)}) fusion(f32[2,8,8,1024]{3,2,1,0:T(8,128)S(1)} %get-tuple-element.10, f32[2,8,8,1024]{3,2,1,0:T(8,128)S(1)} %get-tuple-element.11, f32[8,1024]{1,0:T(8,128)S(1)} %get-tuple-element.8, f32[2,8,8,1024]{3,2,1,0:T(8,128)S(1)} %get-tuple-element.7, ...), kind=kLoop, calls=%fused_computation | loop fusion | flops 524288 | bytes 3178496 | tf_op jit(solution)/shard_map/sub | solution.py:735

commit v6 on v5

--- a/solution.py
+++ b/solution.py
@@ -384,8 +384,7 @@
     def send_sums(i, sums):
         part = jnp.zeros((8, BLOCK), jnp.float32)
         for k, s in enumerate(sums):
-            both = s[0] + s[1]
-            both = both + pltpu.roll(both, 64, 1)
+            both = s + pltpu.roll(s, 64, 1)
             both = both + pltpu.roll(both, 32, 1)
             part = jnp.where(lane8 >> 5 == k, both, part)
         row = jnp.sum(part, axis=0, keepdims=True)
@@ -405,6 +404,9 @@
 
     def beta_of(size, rr, rq, qq):
         return (rr - 2.0 * size * rq + size * size * qq) / rr
+
+    def halves(sums):
+        return [v[0] + v[1] for v in sums]
 
     def outer(o):
         k0, kq, kz = 4 * o, 4 * o + 1, 4 * o + 2
@@ -433,7 +435,7 @@
                 qq = qq + image * image
             return rr, rq, qq
 
-        sums = lax.fori_loop(0, rows, first_dots, (zero, zero, zero), unroll=2)
+        sums = halves(lax.fori_loop(0, rows, first_dots, (zero, zero, zero), unroll=2))
         keep_ends(kq, q0)
         send_halo(kq, slice(0, 2))
         if o == 0:
@@ -459,24 +461,32 @@
         beta0 = beta_of(size0, rr, rq, qq)
         more = 1.0 + beta0
 
+        def second_vectors(row, cb):
+            r, q, z = r0[row + 1, cb], q0[row + 1, cb], z0[row + 1, cb]
+            res = r - size0 * q
+            return res, res + beta0 * r, more * q - size0 * z
+
         def second(row, carry):
             rr, rq, dq, qq = carry
             for cb in range(nblk):
-                r, q, z = r0[row + 1, cb], q0[row + 1, cb], z0[row + 1, cb]
-                res = r - size0 * q
-                way = res + beta0 * r
-                image = more * q - size0 * z
-                r1[row + 1, cb] = res
-                p1[row + 1, cb] = way
-                q1[row + 1, cb] = image
-                seen[row * nblk + cb] = image
+                res, way, image = second_vectors(row, cb)
                 rr = rr + res * res
                 rq = rq + res * image
                 dq = dq + way * image
                 qq = qq + image * image
             return rr, rq, dq, qq
 
-        send_sums(i1, lax.fori_loop(0, rows, second, (zero,) * 4, unroll=2))
+        part_rr, part_rq, part_dq, part_qq = sums = halves(lax.fori_loop(0, rows, second, (zero,) * 4, unroll=2))
+        send_sums(i1, sums)
+
+        def keep_second(row, carry):
+            for cb in range(nblk):
+                r1[row + 1, cb], p1[row + 1, cb], image = second_vectors(row, cb)
+                q1[row + 1, cb] = image
+                seen[row * nblk + cb] = image
+            return carry
+
+        lax.fori_loop(0, rows, keep_second, 0, unroll=2)
         observe()
         inside(q1, z1)
         wait_halo(kz)
@@ -488,30 +498,55 @@
         if o == 0:
             keep_ends(3, z1)
             send_halo(3)
+
+        def third(row, carry):
+            rw, rz, qw, qz, pw, pz = carry
+            for cb in range(nblk):
+                r, q, p, z = r1[row + 1, cb], q1[row + 1, cb], p1[row + 1, cb], z1[row + 1, cb]
+                w = q0[row + 1, cb] - size0 * z0[row + 1, cb]
+                rw = rw + r * w
+                rz = rz + r * z
+                qw = qw + q * w
+                qz = qz + q * z
+                pw = pw + p * w
+                pz = pz + p * z
+            return rw, rz, qw, qz, pw, pz
+
+        rw, rz, qw, qz, pw, pz = halves(lax.fori_loop(0, rows, third, (zero,) * 6, unroll=2))
         rr, rq, dq, qq = take_sums(i1)
         size1 = rr / dq
         beta1 = beta_of(size1, rr, rq, qq)
-
-        def third(row, carry):
-            rr, dq = carry
-            for cb in range(nblk):
-                q = q1[row + 1, cb]
-                res = r1[row + 1, cb] - size1 * q
-                way = res + beta1 * p1[row + 1, cb]
-                image = ((q0[row + 1, cb] - size0 * z0[row + 1, cb]) - size1 * z1[row + 1, cb]) + beta1 * q
-                r2[row + 1, cb] = res
-                p2[row + 1, cb] = way
-                q2[row + 1, cb] = image
-                rr = rr + res * res
-                dq = dq + way * image
-            return rr, dq
-
-        send_sums(i2, lax.fori_loop(0, rows, third, (zero,) * 2, unroll=2))
-        return size0, beta0, size1, beta1
-
-    size0, beta0, size1, beta1 = outer(0)
-    for c in obs_sends + first_copies:
-        c.wait_send()
+        with_r = rw - size1 * rz + beta1 * part_rq
+        with_q = qw - size1 * qz + beta1 * part_qq
+        with_p = pw - size1 * pz + beta1 * part_dq
+        send_sums(
+            i2,
+            [
+                part_rr - 2.0 * size1 * part_rq + size1 * size1 * part_qq,
+                with_r - size1 * with_q + beta1 * with_p,
+            ],
+        )
+
+        def settle(blocks):
+            def line(row, carry):
+                for cb in blocks:
+                    q, p = q1[row + 1, cb], p1[row + 1, cb]
+                    res = r1[row + 1, cb] - size1 * q
+                    r2[row + 1, cb] = res
+                    p2[row + 1, cb] = res + beta1 * p
+                    w = q0[row + 1, cb] - size0 * z0[row + 1, cb]
+                    q2[row + 1, cb] = (w - size1 * z1[row + 1, cb]) + beta1 * q
+                    moved = size0 * r0[row + 1, cb]
+                    x[row + 1, cb] = (moved if o == 0 else x[row + 1, cb] + moved) + size1 * p
+                return carry
+
+            lax.fori_loop(0, rows, line, 0, unroll=2)
+
+        return size0, beta0, size1, beta1, settle
+
+    size0, beta0, size1, beta1, settle = outer(0)
+    end_blocks = sorted({0, 1, nblk - 1})
+    settle(end_blocks)
 
     def beyond(r, q, q_next):
         res = r - size0 * q
@@ -523,13 +558,6 @@
         for cb in range(nblk):
             x[edge, cb], p2[edge, cb], r2[edge, cb] = beyond(field[0, edge, cb], field[1, edge, cb], q1[edge, cb])
     hx[...], hp[...], hr[...] = beyond(hq[0], hq[1], hq1[...])
-
-    def advance(row, carry):
-        for cb in range(nblk):
-            x[row + 1, cb] = size0 * field[0, row + 1, cb] + size1 * p1[row + 1, cb]
-        return carry
-
-    lax.fori_loop(0, rows, advance, 0)
 
     def add_up(square):
         return jnp.sum(square[0] + square[1], axis=0, keepdims=True)
@@ -557,7 +585,7 @@
         )
 
     blank = jnp.zeros((8, BLOCK), jnp.float32)
-    ends = lax.fori_loop(0, rows, surface_ends, (blank, blank))
+    ends = lax.fori_loop(0, rows, surface_ends, (blank, blank), unroll=4)
     surf_pk[0] = ends[0]
     surf_pk[1] = ends[1]
     surf_copies = [
@@ -568,6 +596,7 @@
     ]
     for c in surf_copies[:2]:
         c.start()
+    settle([cb for cb in range(nblk) if cb not in end_blocks])
 
     def surface_middle(row, carry):
         for cb in range(1, nblk - 1):
@@ -618,14 +647,10 @@
             renew(edge, cb)
     for side in range(2):
         hq[4, side] = (hr[side] - size2 * hw[side]) - extra_of(surf_hq[side]) * (hx[side] + size2 * hp[side])
-    size0, beta0, size1, beta1 = outer(1)
-
-    def advance_last(row, carry):
-        for cb in range(nblk):
-            x[row + 1, cb] = (x[row + 1, cb] + size0 * field[4, row + 1, cb]) + size1 * p1[row + 1, cb]
-        return carry
-
-    lax.fori_loop(0, rows, advance_last, 0)
+    size0, beta0, size1, beta1, settle = outer(1)
+    settle(range(nblk))
+    for c in obs_sends + first_copies:
+        c.wait_send()
     for src, dst in ((x, x_out), (p2, p_out), (r2, r_out), (q2, q_out)):
         for cb in range(nblk):
             for h in range(2):

time: 50.5 us -> 49 us (0.970)
  Pallas kernels: 48.5 us -> 47 us
    pallas_call x1, Pallas kernels: 48.5 us -> 47 us  [shards(): pl.pallas_call(functools.partial(kernel, nlat, nlon), out_shape=(shape,)...]
where the time goes in v6:
time: 49 us; the launch traced here: 48.8 us
  Pallas kernels  47 us (96%)
  other arithmetic  1.19 us (2%)
  between operations  0.64 us (1%)
    pallas_call x1, Pallas kernels, shards(): pl.pallas_call(functools.partial(kernel, nlat, nlon), out_shape=(shape,)...  47 us
    sub x1, other arithmetic, shards(): r - size * q  1.19 us

profile of v6, /device:TPU:0, one launch (start us, length us, event | category | flops | bytes accessed | tf_op | source)
XLA Modules:
  0.0 48.8 jit_solution(12440821374677034167)
XLA Ops:
  0.6 47.0 %shard_map.113 = (f32[2,8,8,1024]{3,2,1,0:T(8,128)S(1)}, f32[2,8,8,1024]{3,2,1,0:T(8,128)S(1)}, f32[2,8,8,1024]{3,2,1,0:T(8,128)S(1)}, f32[2,8,8,1024]{3,2,1,0:T(8,128)S(1)}, f32[8,1024]{1,0:T(8,128)S(1)}) custom-call(s32[16]{0:T(128)} %bitcast.7, s32[16]{0:T(128)} %tblk_in.1, f32[8,1024]{1,0:T(8,128)} %depth_in.1, f32[8,1024]{1,0:T(8,128)} %fric_in.1, ...), custom_call_target="tpu_custom_call" | custom-call | tf_op jit(solution)/shard_map/pallas_call | solution.py:747
  47.6 1.2 %multiply_subtract_fusion = (f32[2,8,8,1024]{3,2,1,0:T(8,128)}, f32[2,8,8,1024]{3,2,1,0:T(8,128)}) fusion(f32[2,8,8,1024]{3,2,1,0:T(8,128)S(1)} %get-tuple-element.10, f32[2,8,8,1024]{3,2,1,0:T(8,128)S(1)} %get-tuple-element.11, f32[8,1024]{1,0:T(8,128)S(1)} %get-tuple-element.8, f32[2,8,8,1024]{3,2,1,0:T(8,128)S(1)} %get-tuple-element.7, ...), kind=kLoop, calls=%fused_computation | loop fusion | flops 524288 | bytes 3178496 | tf_op jit(solution)/shard_map/sub | solution.py:760

commit v7 on v6

--- a/solution.py
+++ b/solution.py
@@ -44,7 +44,7 @@
     dw, dwn, dws, dwe, dww, wetfric, coef, diag,
     pay, payi, outf, outi, inf, ini, plan, splan, waves, mats, oslot,
     field, seen, r1, p1, q1, z_last, r2, p2, q2, x,
-    pk, hq, hq1, hx, hp, hr, hw, surf, surf_pk, surf_hq, sum_a, part_row, ready,
+    pk, hq, hq1, hx, hp, hr, hw, surf, surf_pk, surf_hq, near, end_coef, sum_a, part_row, ready,
     load, hs, hrv, ss, sr, as_, ar, os_, orv, ds_, dr, loc,
 ):
     rows, cols = depth.shape
@@ -214,6 +214,12 @@
                 moved = pltpu.roll(src[row + 1, cb], (row + side) % BLOCK, 2)
                 packed = jnp.where(lane8 == row, moved, packed)
             pk[k, side] = packed
+
+    def keep_near(k):
+        packed = zero
+        for row in range(rows):
+            packed = jnp.where(lane8 == row, pltpu.roll(field[k, row + 1, 0], (row + BLOCK - 1) % BLOCK, 2), packed)
+        near[k] = packed
 
     def start_rhs(blocks):
         def line(row, carry):
@@ -278,6 +284,14 @@
         wide = jnp.broadcast_to(wet[row : row + 1], (8, cols))
         diag[row] = wide * stiff + jnp.broadcast_to(total[row : row + 1], (8, cols))
 
+    def pack_rows(ref, lead, side):
+        packed = jnp.zeros((8, BLOCK), jnp.float32)
+        at = pl.ds(side * (cols - BLOCK), BLOCK)
+        for row in range(rows):
+            value = ref[lead + (row, slice(None), at)]
+            packed = jnp.where(lane8 == row, pltpu.roll(value, (row + side) % BLOCK, 1), packed)
+        return packed
+
     def build(o, carry):
         for k in range(CAP):
             weight = inf[o, pl.ds(4 * k + 2, 1), :]
@@ -299,6 +313,10 @@
         return carry
 
     lax.fori_loop(0, slots, join_mats, 0)
+    for side in range(2):
+        end_coef[side, 0] = pack_rows(coef, (0,), side)
+        end_coef[side, 1] = pack_rows(coef, (2,), side)
+        end_coef[side, 2] = pack_rows(wetfric, (), side)
 
     def observe():
         def slot(s, carry):
@@ -442,6 +460,9 @@
             pl.semaphore_wait(ready, nlat - 1)
         send_sums(i0, sums)
         send_halo(kq, slice(2, 4))
+        if o == 0:
+            keep_near(0)
+            keep_near(1)
 
         def look(row, carry):
             for cb in range(nblk):
@@ -456,6 +477,8 @@
 
         keep_ends(kz, z0)
         send_halo(kz)
+        if o == 0:
+            keep_near(2)
         rr, rq, qq, _ = take_sums(i0)
         size0 = rr / rq
         beta0 = beta_of(size0, rr, rq, qq)
@@ -467,16 +490,20 @@
             return res, res + beta0 * r, more * q - size0 * z
 
         def second(row, carry):
-            rr, rq, dq, qq = carry
+            ri, qi, ii = carry
             for cb in range(nblk):
-                res, way, image = second_vectors(row, cb)
-                rr = rr + res * res
-                rq = rq + res * image
-                dq = dq + way * image
-                qq = qq + image * image
-            return rr, rq, dq, qq
-
-        part_rr, part_rq, part_dq, part_qq = sums = halves(lax.fori_loop(0, rows, second, (zero,) * 4, unroll=2))
+                q = q0[row + 1, cb]
+                image = more * q - size0 * z0[row + 1, cb]
+                ri = ri + r0[row + 1, cb] * image
+                qi = qi + q * image
+                ii = ii + image * image
+            return ri, qi, ii
+
+        part_ri, part_qi, part_qq = halves(lax.fori_loop(0, rows, second, (zero,) * 3, unroll=2))
+        part_rr = sums[0] - 2.0 * size0 * sums[1] + size0 * size0 * sums[2]
+        part_rq = part_ri - size0 * part_qi
+        part_dq = part_rq + beta0 * part_ri
+        sums = (part_rr, part_rq, part_dq, part_qq)
         send_sums(i1, sums)
 
         def keep_second(row, carry):
@@ -545,8 +572,6 @@
         return size0, beta0, size1, beta1, settle
 
     size0, beta0, size1, beta1, settle = outer(0)
-    end_blocks = sorted({0, 1, nblk - 1})
-    settle(end_blocks)
 
     def beyond(r, q, q_next):
         res = r - size0 * q
@@ -554,40 +579,32 @@
         res = res - size1 * q_next
         return size0 * r + size1 * way, res + beta1 * way, res
 
-    for edge in (0, rows + 1):
-        for cb in range(nblk):
-            x[edge, cb], p2[edge, cb], r2[edge, cb] = beyond(field[0, edge, cb], field[1, edge, cb], q1[edge, cb])
     hx[...], hp[...], hr[...] = beyond(hq[0], hq[1], hq1[...])
 
     def add_up(square):
         return jnp.sum(square[0] + square[1], axis=0, keepdims=True)
 
-    def surface(row, cb):
-        at = pl.ds(cb * BLOCK, BLOCK)
-        flux = []
-        for ref, halos in ((x, hx), (p2, hp)):
-            v = ref[row + 1, cb]
-            after = pltpu.roll(ref[row + 1, cb + 1], BLOCK - 1, 2) if cb < nblk - 1 else from_east(halos, row)
-            e = jnp.where(lane8 == BLOCK - 1, after, pltpu.roll(v, BLOCK - 1, 2))
-            flux.append((coef[0, row, :, at] * (e - v), coef[2, row, :, at] * (ref[row + 2, cb] - v)))
+    def parts_of(flux, dragged):
         (xe, xn), (pe, pn) = flux
-        parts = jnp.where(sub8 == 0, add_up(xe * xe + xn * xn), wetfric[row, :, at])
+        parts = jnp.where(sub8 == 0, add_up(xe * xe + xn * xn), dragged)
         parts = jnp.where(sub8 == 1, add_up(xe * pe + xn * pn), parts)
-        parts = jnp.where(sub8 == 2, add_up(pe * pe + pn * pn), parts)
-        surf[row + 1, :, at] = parts
-        return parts
-
-    def surface_ends(row, ends):
-        first, last = surface(row, 0), surface(row, nblk - 1)
-        return (
-            jnp.where(lane8 == row, pltpu.roll(first, row, 1), ends[0]),
-            jnp.where(lane8 == row, pltpu.roll(last, row + 1, 1), ends[1]),
-        )
-
-    blank = jnp.zeros((8, BLOCK), jnp.float32)
-    ends = lax.fori_loop(0, rows, surface_ends, (blank, blank), unroll=4)
-    surf_pk[0] = ends[0]
-    surf_pk[1] = ends[1]
+        return jnp.where(sub8 == 2, add_up(pe * pe + pn * pn), parts)
+
+    def extended(k, side):
+        corner = field[k, rows + 1, side * (nblk - 1)]
+        return jnp.where(lane8 == rows, pltpu.roll(corner, (rows + side) % BLOCK, 2), pk[k, side])
+
+    def state(r, q, z):
+        return beyond(r, q, (1.0 + beta0) * q - size0 * z)[:2]
+
+    for side in range(2):
+        own = state(*(extended(k, side) for k in range(3)))
+        after = (hx[1], hp[1]) if side else state(near[0], near[1], near[2])
+        flux = [
+            (end_coef[side, 0] * (e - v), end_coef[side, 1] * (pltpu.roll(v, BLOCK - 1, 2) - v))
+            for v, e in zip(own, after)
+        ]
+        surf_pk[side] = parts_of(flux, end_coef[side, 2])
     surf_copies = [
         remote(surf_pk.at[0], surf_hq.at[1], ss.at[2], sr.at[2], {"lon": west}),
         remote(surf_pk.at[1], surf_hq.at[0], ss.at[3], sr.at[3], {"lon": east}),
@@ -596,14 +613,24 @@
     ]
     for c in surf_copies[:2]:
         c.start()
-    settle([cb for cb in range(nblk) if cb not in end_blocks])
-
-    def surface_middle(row, carry):
-        for cb in range(1, nblk - 1):
-            surface(row, cb)
+    settle(range(nblk))
+    for edge in (0, rows + 1):
+        for cb in range(nblk):
+            x[edge, cb], p2[edge, cb], r2[edge, cb] = beyond(field[0, edge, cb], field[1, edge, cb], q1[edge, cb])
+
+    def surface(row, carry):
+        for cb in range(nblk):
+            at = pl.ds(cb * BLOCK, BLOCK)
+            flux = []
+            for ref, halos in ((x, hx), (p2, hp)):
+                v = ref[row + 1, cb]
+                after = pltpu.roll(ref[row + 1, cb + 1], BLOCK - 1, 2) if cb < nblk - 1 else from_east(halos, row)
+                e = jnp.where(lane8 == BLOCK - 1, after, pltpu.roll(v, BLOCK - 1, 2))
+                flux.append((coef[0, row, :, at] * (e - v), coef[2, row, :, at] * (ref[row + 2, cb] - v)))
+            surf[row + 1, :, at] = parts_of(flux, wetfric[row, :, at])
         return carry
 
-    lax.fori_loop(0, rows, surface_middle, 0)
+    lax.fori_loop(0, rows, surface, 0)
     for c in surf_copies[2:]:
         c.start()
     wait_halo(3)
@@ -727,6 +754,8 @@
         vmem((rows + 2, 8, cols), f32),
         vmem((2, 8, BLOCK), f32),
         vmem((2, 8, BLOCK), f32),
+        vmem((3, 2, 8, BLOCK), f32),
+        vmem((2, 3, 8, BLOCK), f32),
         vmem((SUMS, nlat * nlon, BLOCK), f32),
         vmem((SUMS, 1, BLOCK), f32),
         pltpu.SemaphoreType.REGULAR,

time: 49 us -> 48.4 us (0.988)
  Pallas kernels: 47 us -> 46.4 us
    pallas_call x1, Pallas kernels: 47 us -> 46.4 us  [shards(): pl.pallas_call(functools.partial(kernel, nlat, nlon), out_shape=(shape,)...]
where the time goes in v7:
time: 48.4 us; the launch traced here: 48.2 us
  Pallas kernels  46.4 us (96%)
  other arithmetic  1.19 us (2%)
  between operations  0.64 us (1%)
    pallas_call x1, Pallas kernels, shards(): pl.pallas_call(functools.partial(kernel, nlat, nlon), out_shape=(shape,)...  46.4 us
    sub x1, other arithmetic, shards(): r - size * q  1.19 us

profile of v7, /device:TPU:0, one launch (start us, length us, event | category | flops | bytes accessed | tf_op | source)
XLA Modules:
  0.0 48.2 jit_solution(4958489961130287368)
XLA Ops:
  0.6 46.4 %shard_map.113 = (f32[2,8,8,1024]{3,2,1,0:T(8,128)S(1)}, f32[2,8,8,1024]{3,2,1,0:T(8,128)S(1)}, f32[2,8,8,1024]{3,2,1,0:T(8,128)S(1)}, f32[2,8,8,1024]{3,2,1,0:T(8,128)S(1)}, f32[8,1024]{1,0:T(8,128)S(1)}) custom-call(s32[16]{0:T(128)} %bitcast.7, s32[16]{0:T(128)} %tblk_in.1, f32[8,1024]{1,0:T(8,128)} %depth_in.1, f32[8,1024]{1,0:T(8,128)} %fric_in.1, ...), custom_call_target="tpu_custom_call" | custom-call | tf_op jit(solution)/shard_map/pallas_call | solution.py:776
  47.0 1.2 %multiply_subtract_fusion = (f32[2,8,8,1024]{3,2,1,0:T(8,128)}, f32[2,8,8,1024]{3,2,1,0:T(8,128)}) fusion(f32[2,8,8,1024]{3,2,1,0:T(8,128)S(1)} %get-tuple-element.10, f32[2,8,8,1024]{3,2,1,0:T(8,128)S(1)} %get-tuple-element.11, f32[8,1024]{1,0:T(8,128)S(1)} %get-tuple-element.8, f32[2,8,8,1024]{3,2,1,0:T(8,128)S(1)} %get-tuple-element.7, ...), kind=kLoop, calls=%fused_computation | loop fusion | flops 524288 | bytes 3178496 | tf_op jit(solution)/shard_map/sub | solution.py:789

commit v8 on v7

--- a/solution.py
+++ b/solution.py
@@ -105,19 +105,18 @@
     lax.fori_loop(0, nlon, pick, 0)
     pl.semaphore_wait(barrier, nlon + nlat - 2)
 
-    def obs_copy(k):
+    def obs_copy(n, k):
+        src, dst = ((outi, ini), (outf, inf))[n]
         peer = lax.rem(me_lon + k, nlon)
-        return [
-            remote(outf.at[peer], inf.at[me_lon], os_.at[0, peer], orv.at[0, me_lon], {"lon": peer}),
-            remote(outi.at[peer], ini.at[me_lon], os_.at[1, peer], orv.at[1, me_lon], {"lon": peer}),
-        ]
-
-    def obs_wait(k):
-        peer = lax.rem(me_lon + k, nlon)
-        remote(outf.at[peer], inf.at[peer], os_.at[0, peer], orv.at[0, peer], {"lon": peer}).wait_recv()
-        remote(outi.at[peer], ini.at[peer], os_.at[1, peer], orv.at[1, peer], {"lon": peer}).wait_recv()
-
-    obs_sends = [c for k in range(1, nlon) for c in obs_copy(k)]
+        return remote(src.at[peer], dst.at[me_lon], os_.at[n, peer], orv.at[n, me_lon], {"lon": peer})
+
+    def obs_wait(n):
+        src, dst = ((outi, ini), (outf, inf))[n]
+        for k in range(1, nlon):
+            peer = lax.rem(me_lon + k, nlon)
+            remote(src.at[peer], dst.at[peer], os_.at[n, peer], orv.at[n, peer], {"lon": peer}).wait_recv()
+
+    obs_sends = [obs_copy(n, k) for n in range(2) for k in range(1, nlon)]
     for c in obs_sends:
         c.start()
     first_copies = [
@@ -150,21 +149,17 @@
         rate = jnp.where(sub8 == c, float(RATES[c]), rate)
     cells = lax.broadcasted_iota(jnp.int32, (BLOCK, BLOCK), 0)
 
-    for k in range(1, nlon):
-        obs_wait(k)
-
-    def where_is(s):
-        return ini[s // CAP, pl.ds(s % CAP, 1), :]
-
+    obs_wait(0)
+    places = [ini[s // CAP, pl.ds(s % CAP, 1), :] >> 7 for s in range(slots)]
     rep = jnp.full((1, BLOCK), slots, jnp.int32)
     homes = jnp.full((1, BLOCK), -1, jnp.int32)
     for s in reversed(range(slots)):
-        home = where_is(s) >> 7
+        home = places[s]
         rep = jnp.where(home == lane, s, rep)
         homes = jnp.where(lane == s, home, homes)
     chain = jnp.full((1, BLOCK), slots, jnp.int32)
     for s in reversed(range(slots)):
-        home = where_is(s) >> 7
+        home = places[s]
         chain = jnp.where((home == homes) & (lane < s), s, chain)
     plan[...] = jnp.where(
         sub8 == 0,
@@ -173,6 +168,7 @@
     )
     to_scalars = pltpu.make_async_copy(plan, splan, loc.at[0])
     to_scalars.start()
+    obs_wait(1)
 
     def onto_cells(o, k, terms):
         cell = ini[o, pl.ds(k, 1), :] & (BLOCK - 1)
@@ -246,8 +242,8 @@
         for c in halo(k)[part]:
             c.start()
 
-    def wait_halo(k):
-        for c in halo(k):
+    def wait_halo(k, part=slice(None)):
+        for c in halo(k)[part]:
             c.wait_recv()
 
     send_halo(0, slice(0, 2))
@@ -328,7 +324,7 @@
             oslot[s] = acc[0] + acc[1]
             return carry
 
-        lax.fori_loop(0, slots, slot, 0, unroll=2)
+        lax.fori_loop(0, slots, slot, 0, unroll=4)
 
     def eastward(v, beyond):
         moved = [pltpu.roll(b, BLOCK - 1, 2) for b in v] + [beyond]
@@ -377,18 +373,29 @@
         put(0, image_row(src, 0, zero, zero, to_south=False)[1])
         put(rows - 1, image_row(src, rows - 1, zero, zero, to_north=False)[1])
 
-    def edges(src, halos, dst):
+    def lat_edges(src, dst):
         for cb in range(nblk):
             at = pl.ds(cb * BLOCK, BLOCK)
             dst[1, cb] = dst[1, cb] - coef[3, 0, :, at] * src[0, cb]
             dst[rows, cb] = dst[rows, cb] - coef[2, rows - 1, :, at] * src[rows + 1, cb]
 
-        first, last = pl.ds(0, BLOCK), pl.ds(cols - BLOCK, BLOCK)
+    def lon_edges(src, halos, dst):
+        rq, qq = zero, zero
         for row in range(rows):
-            beside = jnp.where(lane8 == 0, from_west(halos, row), 0.0)
-            dst[row + 1, 0] = dst[row + 1, 0] - coef[1, row, :, first] * beside
-            beside = jnp.where(lane8 == BLOCK - 1, from_east(halos, row), 0.0)
-            dst[row + 1, nblk - 1] = dst[row + 1, nblk - 1] - coef[0, row, :, last] * beside
+            for side in range(2):
+                cb = side * (nblk - 1)
+                beyond = from_east(halos, row) if side else from_west(halos, row)
+                at = pl.ds(cb * BLOCK, BLOCK)
+                change = coef[1 - side, row, :, at] * jnp.where(lane8 == side * (BLOCK - 1), -beyond, 0.0)
+                old = dst[row + 1, cb]
+                dst[row + 1, cb] = old + change
+                rq = rq + src[row + 1, cb] * change
+                qq = qq + change * (old + old + change)
+        return rq, qq
+
+    def edges(src, halos, dst):
+        lat_edges(src, dst)
+        lon_edges(src, halos, dst)
 
     lat_order = sorted(range(nlat), key=lambda k: (k == 0, abs(k - nlat // 2)))
     lon_order = sorted(range(nlon), key=lambda k: (k == 0, k % 2 == 0, -abs(k - nlon // 2)))
@@ -434,8 +441,8 @@
         observe()
         if o == 0:
             inside(r0, q0)
-            wait_halo(k0)
-            edges(r0, hq.at[k0], q0)
+            wait_halo(k0, slice(2, 4))
+            lat_edges(r0, q0)
 
         def first_dots(row, carry):
             rr, rq, qq = carry
@@ -453,7 +460,11 @@
                 qq = qq + image * image
             return rr, rq, qq
 
-        sums = halves(lax.fori_loop(0, rows, first_dots, (zero, zero, zero), unroll=2))
+        sums = halves(lax.fori_loop(0, rows, first_dots, (zero, zero, zero), unroll=rows))
+        if o == 0:
+            wait_halo(k0, slice(0, 2))
+            more_rq, more_qq = halves(lon_edges(r0, hq.at[k0], q0))
+            sums = [sums[0], sums[1] + more_rq, sums[2] + more_qq]
         keep_ends(kq, q0)
         send_halo(kq, slice(0, 2))
         if o == 0:
@@ -499,7 +510,7 @@
                 ii = ii + image * image
             return ri, qi, ii
 
-        part_ri, part_qi, part_qq = halves(lax.fori_loop(0, rows, second, (zero,) * 3, unroll=2))
+        part_ri, part_qi, part_qq = halves(lax.fori_loop(0, rows, second, (zero,) * 3, unroll=4))
         part_rr = sums[0] - 2.0 * size0 * sums[1] + size0 * size0 * sums[2]
         part_rq = part_ri - size0 * part_qi
         part_dq = part_rq + beta0 * part_ri
@@ -668,7 +679,7 @@
             seen[row * nblk + cb] = new
         return carry
 
-    lax.fori_loop(0, rows, friction, 0, unroll=2)
+    lax.fori_loop(0, rows, friction, 0, unroll=4)
     for edge in (0, rows + 1):
         for cb in range(nblk):
             renew(edge, cb)

time: 48.4 us -> 47.8 us (0.988)
  Pallas kernels: 46.4 us -> 45.8 us
    pallas_call x1, Pallas kernels: 46.4 us -> 45.8 us  [shards(): pl.pallas_call(functools.partial(kernel, nlat, nlon), out_shape=(shape,)...]
where the time goes in v8:
time: 47.8 us; the launch traced here: 47.6 us
  Pallas kernels  45.8 us (96%)
  other arithmetic  1.19 us (2%)
  between operations  0.64 us (1%)
    pallas_call x1, Pallas kernels, shards(): pl.pallas_call(functools.partial(kernel, nlat, nlon), out_shape=(shape,)...  45.8 us
    sub x1, other arithmetic, shards(): r - size * q  1.19 us

profile of v8, /device:TPU:0, one launch (start us, length us, event | category | flops | bytes accessed | tf_op | source)
XLA Modules:
  0.0 47.6 jit_solution(8539335753924639059)
XLA Ops:
  0.6 45.8 %shard_map.113 = (f32[2,8,8,1024]{3,2,1,0:T(8,128)S(1)}, f32[2,8,8,1024]{3,2,1,0:T(8,128)S(1)}, f32[2,8,8,1024]{3,2,1,0:T(8,128)S(1)}, f32[2,8,8,1024]{3,2,1,0:T(8,128)S(1)}, f32[8,1024]{1,0:T(8,128)S(1)}) custom-call(s32[16]{0:T(128)} %bitcast.7, s32[16]{0:T(128)} %tblk_in.1, f32[8,1024]{1,0:T(8,128)} %depth_in.1, f32[8,1024]{1,0:T(8,128)} %fric_in.1, ...), custom_call_target="tpu_custom_call" | custom-call | tf_op jit(solution)/shard_map/pallas_call | solution.py:787
  46.4 1.2 %multiply_subtract_fusion = (f32[2,8,8,1024]{3,2,1,0:T(8,128)}, f32[2,8,8,1024]{3,2,1,0:T(8,128)}) fusion(f32[2,8,8,1024]{3,2,1,0:T(8,128)S(1)} %get-tuple-element.10, f32[2,8,8,1024]{3,2,1,0:T(8,128)S(1)} %get-tuple-element.11, f32[8,1024]{1,0:T(8,128)S(1)} %get-tuple-element.8, f32[2,8,8,1024]{3,2,1,0:T(8,128)S(1)} %get-tuple-element.7, ...), kind=kLoop, calls=%fused_computation | loop fusion | flops 524288 | bytes 3178496 | tf_op jit(solution)/shard_map/sub | solution.py:800

commit v9 on v8

--- a/solution.py
+++ b/solution.py
@@ -39,7 +39,7 @@
 def kernel(
     nlat, nlon,
     route_in, tblk_in, depth_in, fric_in, mask_in, forc_in, ocell_in, otime_in, oval_in, oweight_in,
-    x_out, p_out, r_out, q_out, size_out,
+    x_out, p_out, r_out, q_out, w_out, z_out, first_out, second_out, third_out,
     route, tblk, depth, fric, mask, forc, ocell, otime, oval, oweight,
     dw, dwn, dws, dwe, dww, wetfric, coef, diag,
     pay, payi, outf, outi, inf, ini, plan, splan, waves, mats, oslot,
@@ -379,8 +379,8 @@
             dst[1, cb] = dst[1, cb] - coef[3, 0, :, at] * src[0, cb]
             dst[rows, cb] = dst[rows, cb] - coef[2, rows - 1, :, at] * src[rows + 1, cb]
 
-    def lon_edges(src, halos, dst):
-        rq, qq = zero, zero
+    def lon_edges(halos, dst, refs=()):
+        dots, square = [zero] * len(refs), zero
         for row in range(rows):
             for side in range(2):
                 cb = side * (nblk - 1)
@@ -389,13 +389,9 @@
                 change = coef[1 - side, row, :, at] * jnp.where(lane8 == side * (BLOCK - 1), -beyond, 0.0)
                 old = dst[row + 1, cb]
                 dst[row + 1, cb] = old + change
-                rq = rq + src[row + 1, cb] * change
-                qq = qq + change * (old + old + change)
-        return rq, qq
-
-    def edges(src, halos, dst):
-        lat_edges(src, dst)
-        lon_edges(src, halos, dst)
+                dots = [dot + ref[row + 1, cb] * change for dot, ref in zip(dots, refs)]
+                square = square + change * (old + old + change)
+        return [v[0] + v[1] for v in dots + [square]]
 
     lat_order = sorted(range(nlat), key=lambda k: (k == 0, abs(k - nlat // 2)))
     lon_order = sorted(range(nlon), key=lambda k: (k == 0, k % 2 == 0, -abs(k - nlon // 2)))
@@ -408,10 +404,13 @@
 
     def send_sums(i, sums):
         part = jnp.zeros((8, BLOCK), jnp.float32)
+        groups = 4 if len(sums) <= 4 else 16
         for k, s in enumerate(sums):
-            both = s + pltpu.roll(s, 64, 1)
-            both = both + pltpu.roll(both, 32, 1)
-            part = jnp.where(lane8 >> 5 == k, both, part)
+            both, wide = s, BLOCK
+            while wide * groups > BLOCK:
+                wide = wide // 2
+                both = both + pltpu.roll(both, wide, 1)
+            part = jnp.where(lane8 // (BLOCK // groups) == k, both, part)
         row = jnp.sum(part, axis=0, keepdims=True)
         part_row[i] = row
         sum_a[i, pl.ds(me, 1)] = row
@@ -421,17 +420,26 @@
                     where = {"lat": lat_peers[a], "lon": lon_peers[b]}
                     remote(part_row.at[i], sum_a.at[i, pl.ds(me, 1)], as_.at[i], ar.at[i], where).start()
 
-    def take_sums(i):
+    def take_sums(i, number=4):
         sum_wait(i).wait_recv()
+        groups, tall = (4, 8) if number <= 4 else (16, 16)
         total = jnp.sum(sum_a[i], axis=0, keepdims=True)
-        whole = jnp.sum(jnp.where(lane8 >> 5 == sub8, total, 0.0), axis=1, keepdims=True)
-        return [jnp.broadcast_to(whole[k : k + 1], (8, BLOCK)) for k in range(4)]
+        lanes = lax.broadcasted_iota(jnp.int32, (tall, BLOCK), 1) // (BLOCK // groups)
+        own = lanes == lax.broadcasted_iota(jnp.int32, (tall, BLOCK), 0)
+        whole = jnp.sum(jnp.where(own, total, 0.0), axis=1, keepdims=True)
+        return [jnp.broadcast_to(whole[k : k + 1], (8, BLOCK)) for k in range(number)]
 
     def beta_of(size, rr, rq, qq):
         return (rr - 2.0 * size * rq + size * size * qq) / rr
 
     def halves(sums):
         return [v[0] + v[1] for v in sums]
+
+    def last_sums(size, beta, rr, rq, dq, qq, rw, rz, qw, qz, pw, pz):
+        with_r = rw - size * rz + beta * rq
+        with_q = qw - size * qz + beta * qq
+        with_p = pw - size * pz + beta * dq
+        return [rr - 2.0 * size * rq + size * size * qq, with_r - size * with_q + beta * with_p]
 
     def outer(o):
         k0, kq, kz = 4 * o, 4 * o + 1, 4 * o + 2
@@ -463,7 +471,7 @@
         sums = halves(lax.fori_loop(0, rows, first_dots, (zero, zero, zero), unroll=rows))
         if o == 0:
             wait_halo(k0, slice(0, 2))
-            more_rq, more_qq = halves(lon_edges(r0, hq.at[k0], q0))
+            more_rq, more_qq = lon_edges(hq.at[k0], q0, (r0,))
             sums = [sums[0], sums[1] + more_rq, sums[2] + more_qq]
         keep_ends(kq, q0)
         send_halo(kq, slice(0, 2))
@@ -483,8 +491,10 @@
         lax.fori_loop(0, rows, look, 0)
         observe()
         inside(q0, z0)
-        wait_halo(kq)
-        edges(q0, hq.at[kq], z0)
+        wait_halo(kq, slice(2, 4))
+        lat_edges(q0, z0)
+        wait_halo(kq, slice(0, 2))
+        lon_edges(hq.at[kq], z0)
 
         keep_ends(kz, z0)
         send_halo(kz)
@@ -515,7 +525,8 @@
         part_rq = part_ri - size0 * part_qi
         part_dq = part_rq + beta0 * part_ri
         sums = (part_rr, part_rq, part_dq, part_qq)
-        send_sums(i1, sums)
+        if o == 0:
+            send_sums(i1, sums)
 
         def keep_second(row, carry):
             for cb in range(nblk):
@@ -527,15 +538,11 @@
         lax.fori_loop(0, rows, keep_second, 0, unroll=2)
         observe()
         inside(q1, z1)
-        wait_halo(kz)
+        wait_halo(kz, slice(2, 4))
         for edge in (0, rows + 1):
             for cb in range(nblk):
                 q1[edge, cb] = more * q0[edge, cb] - size0 * z0[edge, cb]
-        hq1[...] = more * hq[kq] - size0 * hq[kz]
-        edges(q1, hq1, z1)
-        if o == 0:
-            keep_ends(3, z1)
-            send_halo(3)
+        lat_edges(q1, z1)
 
         def third(row, carry):
             rw, rz, qw, qz, pw, pz = carry
@@ -551,19 +558,20 @@
             return rw, rz, qw, qz, pw, pz
 
         rw, rz, qw, qz, pw, pz = halves(lax.fori_loop(0, rows, third, (zero,) * 6, unroll=2))
+        wait_halo(kz, slice(0, 2))
+        hq1[...] = more * hq[kq] - size0 * hq[kz]
+        more_rz, more_qz, more_pz, _ = lon_edges(hq1, z1, (r1, q1, p1))
+        rz, qz, pz = rz + more_rz, qz + more_qz, pz + more_pz
+        if o == 0:
+            keep_ends(3, z1)
+            send_halo(3)
+        if o > 0:
+            send_sums(i1, list(sums) + [rw, rz, qw, qz, pw, pz])
+            return size0
         rr, rq, dq, qq = take_sums(i1)
         size1 = rr / dq
         beta1 = beta_of(size1, rr, rq, qq)
-        with_r = rw - size1 * rz + beta1 * part_rq
-        with_q = qw - size1 * qz + beta1 * part_qq
-        with_p = pw - size1 * pz + beta1 * part_dq
-        send_sums(
-            i2,
-            [
-                part_rr - 2.0 * size1 * part_rq + size1 * size1 * part_qq,
-                with_r - size1 * with_q + beta1 * with_p,
-            ],
-        )
+        send_sums(i2, last_sums(size1, beta1, *sums, rw, rz, qw, qz, pw, pz))
 
         def settle(blocks):
             def line(row, carry):
@@ -574,8 +582,7 @@
                     p2[row + 1, cb] = res + beta1 * p
                     w = q0[row + 1, cb] - size0 * z0[row + 1, cb]
                     q2[row + 1, cb] = (w - size1 * z1[row + 1, cb]) + beta1 * q
-                    moved = size0 * r0[row + 1, cb]
-                    x[row + 1, cb] = (moved if o == 0 else x[row + 1, cb] + moved) + size1 * p
+                    x[row + 1, cb] = size0 * r0[row + 1, cb] + size1 * p
                 return carry
 
             lax.fori_loop(0, rows, line, 0, unroll=2)
@@ -685,22 +692,30 @@
             renew(edge, cb)
     for side in range(2):
         hq[4, side] = (hr[side] - size2 * hw[side]) - extra_of(surf_hq[side]) * (hx[side] + size2 * hp[side])
-    size0, beta0, size1, beta1, settle = outer(1)
-    settle(range(nblk))
+    size0 = outer(1)
+    for cb in range(nblk):
+        at = pl.ds(cb * BLOCK, BLOCK)
+        for h in range(2):
+            own = (pl.ds(1, rows), cb, h)
+            x_out[h, :, :, at] = jnp.swapaxes(x[own] + size0 * field[(4,) + own], 0, 1)
+            w_out[h, :, :, at] = jnp.swapaxes(field[(5,) + own] - size0 * field[(6,) + own], 0, 1)
+            for src, dst in ((p1, p_out), (r1, r_out), (q1, q_out), (z_last, z_out)):
+                dst[h, :, :, at] = jnp.swapaxes(src[own], 0, 1)
     for c in obs_sends + first_copies:
         c.wait_send()
-    for src, dst in ((x, x_out), (p2, p_out), (r2, r_out), (q2, q_out)):
-        for cb in range(nblk):
-            for h in range(2):
-                dst[h, :, :, pl.ds(cb * BLOCK, BLOCK)] = jnp.swapaxes(src[pl.ds(1, rows), cb, h], 0, 1)
     for k in (0, 1, 2, 3, 5, 6):
         for c in halo(k):
             c.wait_send()
     for c in surf_copies:
         c.wait_send()
-    rr, dq, _, _ = take_sums(SUMS - 1)
-    size_out[...] = jnp.broadcast_to((rr / dq)[:, 0:1], (8, cols))
-    for i in range(SUMS):
+    rr, rq, dq, qq, *others = take_sums(SUMS - 2, 10)
+    size1 = rr / dq
+    beta1 = beta_of(size1, rr, rq, qq)
+    rr, dq = last_sums(size1, beta1, rr, rq, dq, qq, *others)
+    size2 = rr / dq
+    for dst, value in ((first_out, size1 + size2 * beta1), (second_out, size2), (third_out, size1 * size2)):
+        dst[...] = jnp.broadcast_to(value[:, 0:1], (8, cols))
+    for i in range(SUMS - 1):
         sum_wait(i).wait_send()
 
 
@@ -784,20 +799,22 @@
         dma((1,)),
     ]
     shape = vmem(split, f32)
-    x, p, r, q, size = pl.pallas_call(
+    x, p, r, q, w, z, first, second, third = pl.pallas_call(
         functools.partial(kernel, nlat, nlon),
-        out_shape=(shape,) * 4 + (vmem((rows, cols), f32),),
+        out_shape=(shape,) * 6 + (vmem((8, cols), f32),) * 3,
         in_specs=[hbm] * 10,
-        out_specs=(pl.BlockSpec(memory_space=vmem),) * 5,
+        out_specs=(pl.BlockSpec(memory_space=vmem),) * 9,
         scratch_shapes=scratch,
         compiler_params=pltpu.CompilerParams(
-            collective_id=0, has_side_effects=True, vmem_limit_bytes=61 * 2**20
+            collective_id=0, has_side_effects=True, vmem_limit_bytes=60 * 2**20
         ),
     )(
         tile_route.reshape(-1), tile_block, depth, friction, ocean_mask, forcing.reshape(split),
         obs_cell, obs_time, obs_value, obs_weight,
     )
-    return (x + size * p).reshape(forcing.shape), (r - size * q).reshape(forcing.shape)
+    x = x + first * p + second * r - third * q
+    r = r - first * q - second * w + third * z
+    return x.reshape(forcing.shape), r.reshape(forcing.shape)
 
 
 def solution(mesh):

time: 47.8 us -> 47.1 us (0.985)
  Pallas kernels: 45.8 us -> 44.9 us
    add x0 -> x1, other arithmetic: none -> 1.39 us  [shards(): r = r - first * q - second * w + third * z]
    sub x1 -> x0, other arithmetic: 1.19 us -> none  [shards(): r - size * q]
    pallas_call x1, Pallas kernels: 45.8 us -> 44.9 us  [shards(): pl.pallas_call(functools.partial(kernel, nlat, nlon), out_shape=(shape,)...]
where the time goes in v9:
time: 47.1 us; the launch traced here: 47 us
  Pallas kernels  44.9 us (95%)
  other arithmetic  1.39 us (3%)
  between operations  0.64 us (1%)
    pallas_call x1, Pallas kernels, shards(): pl.pallas_call(functools.partial(kernel, nlat, nlon), out_shape=(shape,)...  44.9 us
    add x1, other arithmetic, shards(): r = r - first * q - second * w + third * z  1.39 us

profile of v9, /device:TPU:0, one launch (start us, length us, event | category | flops | bytes accessed | tf_op | source)
XLA Modules:
  0.0 47.0 jit_solution(4402975291390977401)
XLA Ops:
  0.6 44.9 %shard_map.113 = (f32[2,8,8,1024]{3,2,1,0:T(8,128)S(1)}, f32[2,8,8,1024]{3,2,1,0:T(8,128)S(1)}, f32[2,8,8,1024]{3,2,1,0:T(8,128)S(1)}, f32[2,8,8,1024]{3,2,1,0:T...) custom-call(s32[16]{0:T(128)} %bitcast.7, ...), custom_call_target="tpu_custom_call" | custom-call | tf_op jit(solution)/shard_map/pallas_call | solution.py:802
  45.6 1.4 %multiply_add_fusion = (f32[2,8,8,1024]{3,2,1,0:T(8,128)}, f32[2,8,8,1024]{3,2,1,0:T(8,128)}) fusion(f32[2,8,8,1024]{3,2,1,0:T(8,128)S(1)} %get-tuple-element.19, f32[2,8,8,1024]{3,2,1,0:T(8,128)S(1)} %get-tuple-element.18, f32[2,8,8,1024]{3,2,1,0:T(8,128)S(1)} %get-tuple-element.15, f32[2,8,8,1024]{3,2,1,0:T(8,128)S(1)} %get-tuple-element.17, ...), kind=kLoop, calls=%fused_computation | loop fusion | flops 1572864 | bytes 4292608 | tf_op jit(solution)/shard_map/add | solution.py:816

commit v10 on v9

--- a/solution.py
+++ b/solution.py
@@ -59,7 +59,8 @@
     count = nlat * nlon
 
     barrier = pltpu.get_barrier_semaphore()
-    for k in range(1, nlon):
+    lon_order = sorted(range(nlon), key=lambda k: (k == 0, k % 2 == 0, -abs(k - nlon // 2)))
+    for k in lon_order[:-1]:
         pl.semaphore_signal(barrier, inc=1, device_id={"lon": lax.rem(me_lon + k, nlon)}, device_id_type=MESH)
     for k in range(1, nlat):
         pl.semaphore_signal(barrier, inc=1, device_id={"lat": lax.rem(me_lat + k, nlat)}, device_id_type=MESH)
@@ -116,7 +117,7 @@
             peer = lax.rem(me_lon + k, nlon)
             remote(src.at[peer], dst.at[peer], os_.at[n, peer], orv.at[n, peer], {"lon": peer}).wait_recv()
 
-    obs_sends = [obs_copy(n, k) for n in range(2) for k in range(1, nlon)]
+    obs_sends = [obs_copy(n, k) for n in range(2) for k in lon_order[:-1]]
     for c in obs_sends:
         c.start()
     first_copies = [
@@ -369,7 +370,7 @@
             put(row, image_row(src, row, zero, zero)[1])
             return carry
 
-        lax.fori_loop(1, rows - 1, line, 0, unroll=2)
+        lax.fori_loop(1, rows - 1, line, 0, unroll=3 if (rows - 2) % 3 == 0 else 2)
         put(0, image_row(src, 0, zero, zero, to_south=False)[1])
         put(rows - 1, image_row(src, rows - 1, zero, zero, to_north=False)[1])
 
@@ -394,7 +395,6 @@
         return [v[0] + v[1] for v in dots + [square]]
 
     lat_order = sorted(range(nlat), key=lambda k: (k == 0, abs(k - nlat // 2)))
-    lon_order = sorted(range(nlon), key=lambda k: (k == 0, k % 2 == 0, -abs(k - nlon // 2)))
     lat_peers = {k: lax.rem(me_lat + k, nlat) for k in lat_order}
     lon_peers = {k: lax.rem(me_lon + k, nlon) for k in lon_order}
 
@@ -474,11 +474,12 @@
             more_rq, more_qq = lon_edges(hq.at[k0], q0, (r0,))
             sums = [sums[0], sums[1] + more_rq, sums[2] + more_qq]
         keep_ends(kq, q0)
-        send_halo(kq, slice(0, 2))
+        send_halo(kq, slice(0, 2) if o == 0 else slice(None))
         if o == 0:
             pl.semaphore_wait(ready, nlat - 1)
         send_sums(i0, sums)
-        send_halo(kq, slice(2, 4))
+        if o == 0:
+            send_halo(kq, slice(2, 4))
         if o == 0:
             keep_near(0)
             keep_near(1)
@@ -535,7 +536,7 @@
                 seen[row * nblk + cb] = image
             return carry
 
-        lax.fori_loop(0, rows, keep_second, 0, unroll=2)
+        lax.fori_loop(0, rows, keep_second, 0, unroll=4)
         observe()
         inside(q1, z1)
         wait_halo(kz, slice(2, 4))
@@ -557,7 +558,7 @@
                 pz = pz + p * z
             return rw, rz, qw, qz, pw, pz
 
-        rw, rz, qw, qz, pw, pz = halves(lax.fori_loop(0, rows, third, (zero,) * 6, unroll=2))
+        rw, rz, qw, qz, pw, pz = halves(lax.fori_loop(0, rows, third, (zero,) * 6, unroll=4))
         wait_halo(kz, slice(0, 2))
         hq1[...] = more * hq[kq] - size0 * hq[kz]
         more_rz, more_qz, more_pz, _ = lon_edges(hq1, z1, (r1, q1, p1))

time: 47.1 us -> 46.9 us (level)
  no operation moved by 1% of the time
where the time goes in v10:
time: 46.9 us; the launch traced here: 46.7 us
  Pallas kernels  44.7 us (95%)
  other arithmetic  1.39 us (3%)
  between operations  0.64 us (1%)
    pallas_call x1, Pallas kernels, shards(): pl.pallas_call(functools.partial(kernel, nlat, nlon), out_shape=(shape,)...  44.7 us
    add x1, other arithmetic, shards(): r = r - first * q - second * w + third * z  1.39 us

profile of v10, /device:TPU:0, one launch (start us, length us, event | category | flops | bytes accessed | tf_op | source)
XLA Modules:
  0.0 46.7 jit_solution(2089732296751480785)
XLA Ops:
  0.6 44.7 %shard_map.113 = (f32[2,8,8,1024]{3,2,1,0:T(8,128)S(1)}, f32[2,8,8,1024]{3,2,1,0:T(8,128)S(1)}, f32[2,8,8,1024]{3,2,1,0:T(8,128)S(1)}, f32[2,8,8,1024]{3,2,1,0:T...) custom-call(s32[16]{0:T(128)} %bitcast.7, ...), custom_call_target="tpu_custom_call" | custom-call | tf_op jit(solution)/shard_map/pallas_call | solution.py:803
  45.4 1.4 %multiply_add_fusion = (f32[2,8,8,1024]{3,2,1,0:T(8,128)}, f32[2,8,8,1024]{3,2,1,0:T(8,128)}) fusion(f32[2,8,8,1024]{3,2,1,0:T(8,128)S(1)} %get-tuple-element.19, f32[2,8,8,1024]{3,2,1,0:T(8,128)S(1)} %get-tuple-element.18, f32[2,8,8,1024]{3,2,1,0:T(8,128)S(1)} %get-tuple-element.15, f32[2,8,8,1024]{3,2,1,0:T(8,128)S(1)} %get-tuple-element.17, ...), kind=kLoop, calls=%fused_computation | loop fusion | flops 1572864 | bytes 4292608 | tf_op jit(solution)/shard_map/add | solution.py:817

commit v11 on v10

--- a/solution.py
+++ b/solution.py
@@ -150,6 +150,30 @@
         rate = jnp.where(sub8 == c, float(RATES[c]), rate)
     cells = lax.broadcasted_iota(jnp.int32, (BLOCK, BLOCK), 0)
 
+    for c in first_copies[2:]:
+        c.wait_recv()
+    a = dw[...]
+    colid = lax.broadcasted_iota(jnp.int32, (rows, cols), 1)
+    rowid = lax.broadcasted_iota(jnp.int32, (rows, cols), 0)
+    keep_n = (me_lat < nlat - 1).astype(jnp.float32)
+    keep_s = (me_lat > 0).astype(jnp.float32)
+
+    def harmonic(first, second):
+        return 2.0 * first * second / jnp.maximum(first + second, 0.5)
+
+    drag = fric[...]
+    total = wet * drag + (1.0 - wet)
+    around = (
+        lambda: jnp.where(colid == cols - 1, dwe[:, 0:1], pltpu.roll(a, cols - 1, 1)),
+        lambda: jnp.where(colid == 0, dww[:, BLOCK - 1 : BLOCK], pltpu.roll(a, 1, 1)),
+        lambda: jnp.where(rowid == rows - 1, dwn[0:1, :] * keep_n, pltpu.roll(a, rows - 1, 0)),
+        lambda: jnp.where(rowid == 0, dws[rows - 1 : rows, :] * keep_s, pltpu.roll(a, 1, 0)),
+    )
+    for k in (2, 3):
+        side = harmonic(a, around[k]())
+        total = total + side
+        for row in range(rows):
+            coef[k, row] = jnp.broadcast_to(side[row : row + 1], (8, cols))
     obs_wait(0)
     places = [ini[s // CAP, pl.ds(s % CAP, 1), :] >> 7 for s in range(slots)]
     rep = jnp.full((1, BLOCK), slots, jnp.int32)
@@ -251,26 +275,9 @@
     start_rhs(range(1, nblk - 1))
     send_halo(0, slice(2, 4))
 
-    for c in first_copies:
+    for c in first_copies[:2]:
         c.wait_recv()
-    a = dw[...]
-    colid = lax.broadcasted_iota(jnp.int32, (rows, cols), 1)
-    rowid = lax.broadcasted_iota(jnp.int32, (rows, cols), 0)
-    keep_n = (me_lat < nlat - 1).astype(jnp.float32)
-    keep_s = (me_lat > 0).astype(jnp.float32)
-
-    def harmonic(first, second):
-        return 2.0 * first * second / jnp.maximum(first + second, 0.5)
-
-    drag = fric[...]
-    total = wet * drag + (1.0 - wet)
-    around = (
-        lambda: jnp.where(colid == cols - 1, dwe[:, 0:1], pltpu.roll(a, cols - 1, 1)),
-        lambda: jnp.where(colid == 0, dww[:, BLOCK - 1 : BLOCK], pltpu.roll(a, 1, 1)),
-        lambda: jnp.where(rowid == rows - 1, dwn[0:1, :] * keep_n, pltpu.roll(a, rows - 1, 0)),
-        lambda: jnp.where(rowid == 0, dws[rows - 1 : rows, :] * keep_s, pltpu.roll(a, 1, 0)),
-    )
-    for k in range(4):
+    for k in (0, 1):
         side = harmonic(a, around[k]())
         total = total + side
         for row in range(rows):

time: 46.9 us -> 46.9 us (level)
  no operation moved by 1% of the time
where the time goes in v11:
time: 46.9 us; the launch traced here: 46.8 us
  Pallas kernels  44.7 us (95%)
  other arithmetic  1.39 us (3%)
  between operations  0.64 us (1%)
    pallas_call x1, Pallas kernels, shards(): pl.pallas_call(functools.partial(kernel, nlat, nlon), out_shape=(shape,)...  44.7 us
    add x1, other arithmetic, shards(): r = r - first * q - second * w + third * z  1.39 us

profile of v11, /device:TPU:0, one launch (start us, length us, event | category | flops | bytes accessed | tf_op | source)
XLA Modules:
  0.0 46.8 jit_solution(8045714659605266780)
XLA Ops:
  0.6 44.7 %shard_map.113 = (f32[2,8,8,1024]{3,2,1,0:T(8,128)S(1)}, f32[2,8,8,1024]{3,2,1,0:T(8,128)S(1)}, f32[2,8,8,1024]{3,2,1,0:T(8,128)S(1)}, f32[2,8,8,1024]{3,2,1,0:T...) custom-call(s32[16]{0:T(128)} %bitcast.7, ...), custom_call_target="tpu_custom_call" | custom-call | tf_op jit(solution)/shard_map/pallas_call | solution.py:810
  45.4 1.4 %multiply_add_fusion = (f32[2,8,8,1024]{3,2,1,0:T(8,128)}, f32[2,8,8,1024]{3,2,1,0:T(8,128)}) fusion(f32[2,8,8,1024]{3,2,1,0:T(8,128)S(1)} %get-tuple-element.19, f32[2,8,8,1024]{3,2,1,0:T(8,128)S(1)} %get-tuple-element.18, f32[2,8,8,1024]{3,2,1,0:T(8,128)S(1)} %get-tuple-element.15, f32[2,8,8,1024]{3,2,1,0:T(8,128)S(1)} %get-tuple-element.17, ...), kind=kLoop, calls=%fused_computation | loop fusion | flops 1572864 | bytes 4292608 | tf_op jit(solution)/shard_map/add | solution.py:824
